TPU v7x, 32 devices: a whole 2x2x4 slice. The times are simulated.
32 devices in a mesh: fsdp: 8 (over z, y), dom: 4 (over x, core).
Axes of the slice: x: 2, y: 2, z: 4, core: 2. Of those that a mesh axis runs over, the one named last changes fastest.
Arguments:
- tokens: bfloat16 [8192, 8192], P(('fsdp', 'dom')), may hold values from -6 to 6
- key_grad: bfloat16 [8192, 512], P(('fsdp', 'dom')), may hold values from -6 to 6
- weight: bfloat16 [8192, 512], P('fsdp'), may hold values from -0.0625 to 0.0625
- master: float32 [8192, 512], P(('fsdp', 'dom')), may hold values from -0.0625 to 0.0625
- moment_one: float32 [8192, 512], P(('fsdp', 'dom')), may hold values from -3 to 3
- moment_two: float32 [8192, 512], P(('fsdp', 'dom')), may hold values from 0.1 to 4
- live: int32 [8, 4], replicated, may hold values from 0 to 1, as said below
- buddy: int32 [4], replicated, may hold values from 0 to 3, as said below
Outputs:
- keys: bfloat16 [8192, 512], P(('fsdp', 'dom'))
- input_grad: bfloat16 [8192, 8192], P(('fsdp', 'dom'))
- new_weight: bfloat16 [8192, 512], P('fsdp')
- new_master: float32 [8192, 512], P(('fsdp', 'dom'))
- new_one: float32 [8192, 512], P(('fsdp', 'dom'))
- new_two: float32 [8192, 512], P(('fsdp', 'dom'))
- held_copy: float32 [3, 8192, 512], P(None, ('fsdp', 'dom'))
Inputs may be any that keep to these rules, and one draw needn't show every extreme that they name: `live`: every column (domain) has at least one 1. A permutation of the domains in a single cycle; no domain is its own buddy; some domain's buddy lies 4 / 2 domains further round.
All inputs are finite; a program needn't handle non-finite values.
Results may differ from a plain program's by a relative error of at most 0.005.
Values may be sent and summed in bfloat16 or wider, within the bound.
No kernel may reach another device: no remote copies, remote signals or barrier semaphores. Data moves between devices by JAX's collectives and lax.ppermute only.
A program may use at most 128 MiB of HBM per device.

v0:
```python
import jax
import jax.numpy as jnp
from jax import lax
from jax.sharding import PartitionSpec as P

STEP = 100


def on_device(tokens, key_grad, weight, master, moment_one, moment_two, live, buddy):
    domains = lax.axis_size("dom")
    member = lax.axis_index("fsdp")
    domain = lax.axis_index("dom")
    xf = tokens.astype(jnp.float32)
    rstd = lax.rsqrt(jnp.mean(xf * xf, axis=1, keepdims=True) + 1e-05)
    hat = xf * rstd
    normed = hat.astype(jnp.bfloat16)
    contract = (((1,), (1,)), ((), ()))
    whole = lax.all_gather(weight, "fsdp", axis=0, tiled=True)
    keys = jnp.dot(normed, whole, preferred_element_type=jnp.float32)
    back = lax.dot_general(key_grad, whole, contract, preferred_element_type=jnp.float32)
    keys = keys.astype(jnp.bfloat16)
    input_grad = (rstd * (back - hat * jnp.mean(back * hat, axis=1, keepdims=True))).astype(
        jnp.bfloat16
    )
    live_float = live.astype(jnp.float32)
    norming = live.shape[0] * live.shape[1] / (jnp.sum(live_float) * tokens.shape[0])
    alive_here = lax.dynamic_index_in_dim(
        lax.dynamic_index_in_dim(live_float, member, 0, keepdims=False), domain, 0, keepdims=False
    )
    scale = alive_here * norming
    product = lax.dot_general(
        normed, key_grad, (((0,), (0,)), ((), ())), preferred_element_type=jnp.float32
    )
    group_part = lax.psum_scatter(product * scale, "fsdp", scatter_dimension=0, tiled=True)
    grad = lax.psum_scatter(group_part, "dom", scatter_dimension=0, tiled=True)
    new_one = 0.9 * moment_one + 0.1 * grad
    new_two = 0.95 * moment_two + 0.05 * grad * grad
    first = 1.0 - 0.9**STEP
    second = 1.0 - 0.95**STEP
    update = new_one / first / (jnp.sqrt(new_two / second) + 1e-08)
    new_master = master - 0.002 * (update + 0.1 * master)
    new_weight = lax.all_gather(new_master.astype(jnp.bfloat16), "dom", axis=0, tiled=True)
    state = jnp.stack((new_master, new_one, new_two))[None]
    slots = jnp.arange(domains, dtype=jnp.int32)
    source = jnp.sum(slots * (buddy == domain).astype(jnp.int32))
    everything = lax.all_gather(state, "dom", axis=0, tiled=True)
    held = lax.dynamic_index_in_dim(everything, source, 0, keepdims=False)
    return (keys, input_grad, new_weight, new_master, new_one, new_two, held)


def solution(mesh):
    placed = (
        P(("fsdp", "dom"), None),
        P(("fsdp", "dom"), None),
        P("fsdp", None),
        P(("fsdp", "dom"), None),
        P(("fsdp", "dom"), None),
        P(("fsdp", "dom"), None),
        P(),
        P(),
    )
    return jax.shard_map(
        on_device,
        mesh=mesh,
        in_specs=placed,
        out_specs=(
            P(("fsdp", "dom"), None),
            P(("fsdp", "dom"), None),
            P("fsdp", None),
            P(("fsdp", "dom"), None),
            P(("fsdp", "dom"), None),
            P(("fsdp", "dom"), None),
            P(None, ("fsdp", "dom"), None),
        ),
        check_vma=False,
    )
```

profile of v0, /device:TPU:0, one launch (start us, length us, event | category | flops | bytes accessed | tf_op | source)
XLA Modules:
  0.0 547.4 jit_solution(17388224101187028933)
XLA Ops:
  7.2 0.0 copy-start
  7.2 0.0 reduce-scatter.3.cloned.1.call-start
  7.2 1.3 convert_reduce_fusion
  8.6 0.7 convert_element_type.23
  9.2 3.1 fusion.7
  13.0 0.6 dynamic_slice.10
  14.3 0.0 copy-done
  14.3 10.4 %convolution_multiply_fusion = f32[8192,512]{1,0:T(8,128)} fusion(bf16[256,512]{1,0:T(8,128)(2,1)S(1)} %copy-done, f32[]{:T(128)S(6)} %mul.86, bf16[256,8192]{1,0:T(8,128)(2,1)} %param.8, f32[256]{0:T(256)S(1)} %add_rsqrt_fusion), kind=kOutput, calls=%fused_computation | convolution fusion | flops 2157969408 | bytes 21234692 | tf_op jit(solution)/shard_map/dot_general | solution.py:31
  24.7 0.0 copy-start.5
  24.7 0.0 copy-start.6
  24.7 0.0 copy-start.7
  24.8 0.0 reduce-scatter.3.cloned.1.call-update
  24.8 0.0 copy-start.8
  24.8 0.0 reduce-scatter.5.cloned.1.call-start
  24.8 285.5 %reduce-scatter.3.cloned.1.call-done = f32[1024,512]{1,0:T(8,128)} async-done(((f32[8192,512]{1,0:T(8,128)}), f32[1024,512]{1,0:T(8,128)}) %reduce-scatter.3.cloned.1.call-update) | async-done | bytes 2097168 | tf_op jit(solution)/shard_map/reduce_scatter | solution.py:34
  310.3 0.0 reduce-scatter.5.cloned.1.call-update
  310.3 0.0 all-gather.5.cloned.1.call-start
  310.4 0.7 all-gather.5.cloned.1.call-update
  311.1 0.0 all-gather.7.cloned.1.call-start
  311.1 32.3 %reduce-scatter.5.cloned.1.call-done = f32[256,512]{1,0:T(8,128)} async-done(((f32[1024,512]{1,0:T(8,128)}), f32[256,512]{1,0:T(8,128)}) %reduce-scatter.5.cloned.1.call-update) | async-done | bytes 524304 | tf_op jit(solution)/shard_map/reduce_scatter | solution.py:35
  343.5 0.0 copy-done.5
  343.5 0.0 copy-done.6
  343.5 0.0 copy-done.7
  343.5 2.2 fusion.16
  345.6 0.0 copy-start.2
  345.6 0.0 copy-start.3
  345.6 0.0 copy-start.4
  345.6 0.0 all-gather.7.cloned.1.call-update
  345.7 0.0 all-gather.9.cloned.1.call-start
  345.7 1.4 pad_maximum_fusion
  347.1 0.0 all-gather.9.cloned.1.call-update
  347.2 0.0 copy-done.8
  347.2 0.6 fusion.15
  349.7 120.8 %all-gather.5.cloned.1.call-done = bf16[8192,512]{1,0:T(8,128)(2,1)} async-done(((bf16[1024,512]{1,0:T(8,128)(2,1)}), bf16[8192,512]{1,0:T(8,128)(2,1)}) %all-gather.5.cloned.1.call-update) | async-done | bytes 8388624 | tf_op jit(solution)/shard_map/all_gather | solution.py:18
  470.6 0.0 copy-start.1
  470.6 7.2 %fusion.3 = (f32[256]{0:T(256)S(1)}, f32[256,8192]{1,0:T(8,128)S(1)}) fusion(bf16[256,8192]{1,0:T(8,128)(2,1)} %param.8, f32[256]{0:T(256)S(1)} %add_rsqrt_fusion, bf16[256,512]{1,0:T(8,128)(2,1)S(1)} %copy-done, bf16[8192,512]{1,0:T(8,128)(2,1)} %all-gather.5.cloned.1.call-done), kind=kOutput, calls=%fused_computation.6 | convolution fusion | flops 2155872000 | bytes 21235712 | tf_op jit(solution)/shard_map/dot_general | solution.py:20
  477.8 0.0 copy-done.2
  477.8 0.0 copy-done.3
  477.8 0.0 copy-done.4
  477.8 0.0 copy-done.1
  477.8 6.5 %fusion.11 = bf16[256,512]{1,0:T(8,128)(2,1)} fusion(bf16[8192,512]{1,0:T(8,128)(2,1)} %all-gather.5.cloned.1.call-done, bf16[256,8192]{1,0:T(8,128)(2,1)S(1)} %copy-done.1, f32[256]{0:T(256)S(1)} %add_rsqrt_fusion), kind=kOutput, calls=%fused_computation.14 | convolution fusion | flops 2153906176 | bytes 12846080 | tf_op jit(solution)/shard_map/dot_general | solution.py:19
  484.4 3.1 fusion.6
  487.5 0.0 all-gather.7.cloned.1.call-done
  487.5 48.4 %all-gather.9.cloned.1.call-done = f32[12,256,512]{2,1,0:T(8,128)} async-done(((f32[3,256,512]{2,1,0:T(8,128)}), f32[12,256,512]{2,1,0:T(8,128)}) %all-gather.9.cloned.1.call-update) | async-done | bytes 6291472 | tf_op jit(solution)/shard_map/all_gather | solution.py:46
  535.9 2.7 dynamic-slice_bitcast_fusion
  538.6 2.3 copy.16
  (2 shorter events, 0.0 us)
Async XLA Ops:
  7.2 7.1 %copy-start = (bf16[256,512]{1,0:T(8,128)(2,1)S(1)}, bf16[256,512]{1,0:T(8,128)(2,1)}, u32[]{:S(2)}) copy-start(bf16[256,512]{1,0:T(8,128)(2,1)} %param.9) | copy-start | bytes 786436
  7.2 303.1 %reduce-scatter.3.cloned.1.call-start = ((), (), s32[]{:S(2)}) async-start(), calls=%async_computation.3 | async-start | bytes 18874368 | tf_op jit(solution)/shard_map/reduce_scatter | solution.py:34
  24.7 318.7 %copy-start.5 = (f32[256,512]{1,0:T(8,128)S(1)}, f32[256,512]{1,0:T(8,128)}, u32[]{:S(2)}) copy-start(f32[256,512]{1,0:T(8,128)} %param.11) | copy-start | bytes 1572868
  24.7 318.7 %copy-start.6 = (f32[256,512]{1,0:T(8,128)S(1)}, f32[256,512]{1,0:T(8,128)}, u32[]{:S(2)}) copy-start(f32[256,512]{1,0:T(8,128)} %param.12) | copy-start | bytes 1572868
  24.7 318.7 %copy-start.7 = (f32[256,512]{1,0:T(8,128)S(1)}, f32[256,512]{1,0:T(8,128)}, u32[]{:S(2)}) copy-start(f32[256,512]{1,0:T(8,128)} %param.13) | copy-start | bytes 1572868
  24.8 322.4 %copy-start.8 = (s32[4]{0:T(128)S(1)}, s32[4]{0:T(128)}, u32[]{:S(2)}) copy-start(s32[4]{0:T(128)} %param.15) | copy-start | bytes 52
  24.8 318.7 %reduce-scatter.5.cloned.1.call-start = ((), (), s32[]{:S(2)}) async-start(), calls=%async_computation.4 | async-start | bytes 2621440 | tf_op jit(solution)/shard_map/reduce_scatter | solution.py:35
  310.3 160.2 %all-gather.5.cloned.1.call-start = ((), (), s32[]{:S(2)}) async-start(), calls=%async_computation.2 | async-start | bytes 9437184 | tf_op jit(solution)/shard_map/all_gather | solution.py:18
  311.1 176.4 %all-gather.7.cloned.1.call-start = ((), (), s32[]{:S(2)}) async-start(), calls=%async_computation.5 | async-start | bytes 1310720 | tf_op jit(solution)/shard_map/all_gather | solution.py:42
  345.6 132.1 %copy-start.2 = (f32[256,512]{1,0:T(8,128)}, f32[256,512]{1,0:T(8,128)S(1)}, u32[]{:S(2)}) copy-start(f32[256,512]{1,0:T(8,128)S(1)} %get-tuple-element.23) | copy-start | bytes 1572868
  345.6 132.2 %copy-start.3 = (f32[256,512]{1,0:T(8,128)}, f32[256,512]{1,0:T(8,128)S(1)}, u32[]{:S(2)}) copy-start(f32[256,512]{1,0:T(8,128)S(1)} %get-tuple-element.24) | copy-start | bytes 1572868
  345.6 132.2 %copy-start.4 = (f32[256,512]{1,0:T(8,128)}, f32[256,512]{1,0:T(8,128)S(1)}, u32[]{:S(2)}) copy-start(f32[256,512]{1,0:T(8,128)S(1)} %get-tuple-element.25) | copy-start | bytes 1572868
  345.7 190.2 %all-gather.9.cloned.1.call-start = ((), (), s32[]{:S(2)}) async-start(), calls=%async_computation.6 | async-start | bytes 7864320 | tf_op jit(solution)/shard_map/all_gather | solution.py:46
  470.6 7.2 %copy-start.1 = (bf16[256,8192]{1,0:T(8,128)(2,1)S(1)}, bf16[256,8192]{1,0:T(8,128)(2,1)}, u32[]{:S(2)}) copy-start(bf16[256,8192]{1,0:T(8,128)(2,1)} %param.8) | copy-start | bytes 12582916
Sparse Core Ops, SparseCore 0:
  24.9 285.3 reduce-scatter.2
  313.0 30.4 reduce-scatter.4
  345.6 124.9 all-gather.4
  472.6 14.8 all-gather.6
  489.5 46.3 all-gather.8
where the time goes:
time: 548 us; the launch traced here: 547 us
  waiting for transfers between devices  488 us (89%)
  matrix products  24.2 us (4%)
  between operations  17.2 us (3%)
  other arithmetic  12.4 us (2%)
  local copies, waits for them, and re-layouts  5.56 us (1%)
    reduce_scatter x1, waiting for transfers between devices, on_device(): lax.psum_scatter(product * scale, 'fsdp', scatter_dimension=0, tiled=True)  285 us
    all_gather x1, waiting for transfers between devices, on_device(): whole = lax.all_gather(weight, 'fsdp', axis=0, tiled=True)  121 us
    all_gather x1, waiting for transfers between devices, on_device(): everything = lax.all_gather(state, 'dom', axis=0, tiled=True)  48.4 us
    reduce_scatter x1, waiting for transfers between devices, on_device(): grad = lax.psum_scatter(group_part, 'dom', scatter_dimension=0, tiled=True)  32.3 us
  transfers between devices with their start and end apart: 5, of which 4 were waited for; matrix products, arithmetic and copies ran while one was open for 4% of the time, Pallas kernels for 0%

commit v1 on v0

v1 whole, which is shorter than its diff:
```python
import jax
import jax.numpy as jnp
from jax import lax
from jax.experimental import pallas as pl
from jax.experimental.pallas import tpu as pltpu
from jax.sharding import Mesh
from jax.sharding import PartitionSpec as P

STEP = 100


def shift(value, axis, by):
    size = lax.axis_size(axis)
    return lax.ppermute(value, axis, [(i, (i + by) % size) for i in range(size)])


def pick(array, index, dim):
    return lax.dynamic_index_in_dim(array, index, dim, keepdims=False)


def scatter_sum(terms, axis, dim):
    size = lax.axis_size(axis)
    here = lax.axis_index(axis)
    arrived = [
        shift(pick(terms, (here + by) % size, dim).astype(jnp.bfloat16), axis, by)
        for by in range(1, size)
    ]
    total = pick(terms, here, dim)
    for term in arrived:
        total = total + term.astype(jnp.float32)
    return total


def gather(value, axis, dim):
    size = lax.axis_size(axis)
    here = lax.axis_index(axis)
    if size == 2:
        other = shift(value, axis, 1)
        first = jnp.where(here == 0, value, other)
        second = jnp.where(here == 0, other, value)
        return jnp.stack((first, second), axis=dim)
    slots = jnp.zeros(value.shape[:dim] + (size,) + value.shape[dim:], value.dtype)
    for by in range(size):
        arrived = shift(value, axis, by) if by else value
        slots = lax.dynamic_update_index_in_dim(slots, arrived, (here - by) % size, dim)
    return slots


def general(tokens, key_grad, weight, master, moment_one, moment_two, live, buddy):
    planes, rows_of, chips, cores = (lax.axis_size(a) for a in ("z", "y", "x", "c"))
    z, y, x, c = (lax.axis_index(a) for a in ("z", "y", "x", "c"))
    member = z * rows_of + y
    domain = x * cores + c
    rows, width = master.shape
    half = rows // 2
    features = tokens.shape[1]

    xf = tokens.astype(jnp.float32)
    rstd = lax.rsqrt(jnp.mean(xf * xf, axis=1, keepdims=True) + 1e-05)
    hat = xf * rstd
    normed = hat.astype(jnp.bfloat16)

    quarter = pick(pick(weight.reshape(chips, cores, rows, width), x, 0), c, 0)
    column = gather(quarter, "z", 0)
    upper = gather(gather(column[:, :half], "y", 1), "x", 2)
    lower = gather(gather(column[:, half:], "x", 1), "y", 1)
    mine = jnp.concatenate((upper, lower), axis=3)
    whole = gather(mine, "c", 3).reshape(features, width)

    live_float = live.astype(jnp.float32)
    norming = live.shape[0] * live.shape[1] / (jnp.sum(live_float) * tokens.shape[0])
    alive_here = pick(pick(live_float, member, 0), domain, 0)
    scale = alive_here * norming
    product = lax.dot_general(
        normed, key_grad, (((0,), (0,)), ((), ())), preferred_element_type=jnp.float32
    )
    terms = (product * scale).reshape(planes, rows_of, chips, cores, rows, width)
    terms = scatter_sum(terms, "c", 3)
    upper_sum = scatter_sum(scatter_sum(terms[:, :, :, :half], "x", 2), "y", 1)
    lower_sum = scatter_sum(scatter_sum(terms[:, :, :, half:], "y", 1), "x", 1)
    grad = scatter_sum(jnp.concatenate((upper_sum, lower_sum), axis=1), "z", 0)

    new_one = 0.9 * moment_one + 0.1 * grad
    new_two = 0.95 * moment_two + 0.05 * grad * grad
    first = 1.0 - 0.9**STEP
    second = 1.0 - 0.95**STEP
    update = new_one / first / (jnp.sqrt(new_two / second) + 1e-08)
    new_master = master - 0.002 * (update + 0.1 * master)

    state = jnp.stack((new_master, new_one, new_two)).astype(jnp.bfloat16)
    states = gather(state, "x", 0)
    new_weight = gather(states[:, 0], "c", 1).reshape(weight.shape)
    slots = jnp.arange(chips * cores, dtype=jnp.int32)
    source = jnp.sum(slots * (buddy == domain).astype(jnp.int32))
    other_source = jnp.sum(slots * (buddy == x * cores + 1 - c).astype(jnp.int32))
    from_core = shift(pick(states, other_source // cores, 0), "c", 1)
    from_column = pick(states, source // cores, 0)
    held = jnp.where(source % cores == c, from_column, from_core).astype(jnp.float32)

    keys = jnp.dot(normed, whole, preferred_element_type=jnp.float32)
    inner = jnp.sum(key_grad.astype(jnp.float32) * keys, axis=1, keepdims=True) / features
    back = lax.dot_general(
        key_grad, whole, (((1,), (1,)), ((), ())), preferred_element_type=jnp.float32
    )
    input_grad = (rstd * (back - hat * inner)).astype(jnp.bfloat16)
    return (keys.astype(jnp.bfloat16), input_grad, new_weight, new_master, new_one, new_two, held)


VMEM = pl.BlockSpec(memory_space=pltpu.VMEM)
SMEM = pl.BlockSpec(memory_space=pltpu.SMEM)
MIB = 2**20


def local(body, outs, flops, traffic, limit, *operands, scalars=0, **more):
    return pl.pallas_call(
        body,
        out_shape=[jax.ShapeDtypeStruct(s, t) for s, t in outs],
        in_specs=[SMEM] * scalars + [VMEM] * (len(operands) - scalars),
        out_specs=[VMEM] * len(outs),
        cost_estimate=pl.CostEstimate(flops=8, bytes_accessed=8, transcendentals=0),
        compiler_params=pltpu.CompilerParams(vmem_limit_bytes=limit * MIB),
        **more,
    )(*operands)


def after(value, *others):
    return lax.optimization_barrier((value, *others))[0]


def place():
    return tuple(lax.axis_index(a) for a in ("z", "y", "x", "c"))


def block_of(planes, by, flip_y, flip_x):
    z, y, x, _ = place()
    z = lax.rem(z + (by + planes) % planes, planes)
    return (z * 2 + (1 - y if flip_y else y)) * 2 + (1 - x if flip_x else x)


def prepare_body(rows, order, tokens, ours, soon, later, rstd_out, held, sems):
    c = lax.axis_index("c")
    many, features = tokens.shape
    step = many // 8

    def rows_in(i):
        span = pl.ds(pl.multiple_of(i * step, step), step)
        return pltpu.make_async_copy(tokens.at[span], held.at[span], sems.at[i])

    for i in range(8):
        rows_in(i).start()
    places = [(by, fy, fx) for by in order for fy in (0, 1) for fx in (0, 1)]

    def part(i, _):
        rows_in(i).wait()
        span = pl.ds(pl.multiple_of(i * step, step), step)
        squares = jnp.zeros((step, 128), jnp.float32)
        for j in range(0, features, 512):
            some = held[span, j : j + 512].astype(jnp.float32)
            some = some * some
            for k in range(0, 512, 128):
                squares = squares + some[:, k : k + 128]
        mean = jnp.sum(squares, axis=1, keepdims=True) / features
        rstd = lax.rsqrt(mean + 1e-05)
        rstd_out[span] = rstd
        for side, outs in ((1 - c, (soon, later)), (c, (ours,))):
            share = len(places) // len(outs)
            for j, flips in enumerate(places):
                start = (block_of(len(order), *flips) * 2 + side) * rows
                columns = pl.ds(pl.multiple_of(start, rows), rows)
                at = j % share * rows
                outs[j // share][span, at : at + rows] = (
                    held[span, columns].astype(jnp.float32) * rstd
                ).astype(jnp.bfloat16)
        return 0

    lax.fori_loop(0, 8, part, 0)


def prepare(tokens, rows, order):
    many, features = tokens.shape
    side = ((many, features // 2), jnp.bfloat16)
    part = ((many, features // 4), jnp.bfloat16)
    return pl.pallas_call(
        lambda *refs: prepare_body(rows, order, *refs),
        out_shape=[jax.ShapeDtypeStruct(s, t) for s, t in (side, part, part, ((many, 1), jnp.float32))],
        in_specs=[pl.BlockSpec(memory_space=pltpu.HBM)],
        out_specs=[VMEM] * 4,
        scratch_shapes=[pltpu.VMEM(tokens.shape, tokens.dtype), pltpu.SemaphoreType.DMA((8,))],
        cost_estimate=pl.CostEstimate(flops=8, bytes_accessed=8, transcendentals=0),
        compiler_params=pltpu.CompilerParams(vmem_limit_bytes=47 * MIB),
    )(tokens)


def flags_body(many, live, flags):
    z, y, x, c = place()
    for row, core in ((0, c), (8, 1 - c)):
        alive = live[x * 2 + core, z * 2 + y]
        flags[row : row + 8] = jnp.full((8, flags.shape[1]), alive).astype(jnp.float32)
    blocks = live.shape[0] * live.shape[1]
    alive = sum(live[i, j] for i in range(live.shape[0]) for j in range(live.shape[1]))
    flags[16:24] = blocks / (jnp.full((8, flags.shape[1]), alive).astype(jnp.float32) * many)


def product(order, by, flip_y, flip_x, lower, rows, cores):
    half = rows // 2
    start = (order.index(by) * 4 + flip_y * 2 + flip_x) * rows + lower * half

    def term(parts, grad, flag):
        share = len(order) * 4 * rows // len(parts)
        at = start % share
        return flag * lax.dot_general(
            parts[start // share][:, at : at + half],
            grad[...],
            (((0,), (0,)), ((), ())),
            preferred_element_type=jnp.float32,
        )

    return sum(term(*core) for core in cores)


def first_body(order, rows, group, flags, ours, theirs, own_grad, their_grad, to_x, to_y):
    cores = (((ours,), own_grad, flags[0:1]), ((theirs, theirs), their_grad, flags[8:9]))
    for i, by in enumerate(group):
        for flip in (0, 1):
            to_x[flip, i] = product(order, by, flip, 1, 0, rows, cores).astype(jnp.bfloat16)
            to_y[flip, i] = product(order, by, 1, flip, 1, rows, cores).astype(jnp.bfloat16)


def second_body(order, rows, group, flags, ours, soon, later, own_grad, their_grad, from_x, from_y, to_y, to_x):
    cores = (((ours,), own_grad, flags[0:1]), ((soon, later), their_grad, flags[8:9]))
    for i, by in enumerate(group):
        upper = product(order, by, 1, 0, 0, rows, cores)
        to_y[i] = (upper + from_x[1, i].astype(jnp.float32)).astype(jnp.bfloat16)
        lower = product(order, by, 0, 1, 1, rows, cores)
        to_x[i] = (lower + from_y[1, i].astype(jnp.float32)).astype(jnp.bfloat16)


def own_half(order, rows, by, i, lower, cores, near, second):
    total = product(order, by, 0, 0, lower, rows, cores)
    return total + near[0, i].astype(jnp.float32) + second[i].astype(jnp.float32)


def third_body(order, rows, group, flags, ours, soon, later, own_grad, their_grad, from_x, from_y, late_y, late_x, *outs):
    cores = (((ours,), own_grad, flags[0:1]), ((soon, later), their_grad, flags[8:9]))
    half = rows // 2
    for i, by in enumerate(group):
        upper = own_half(order, rows, by, i, 0, cores, from_x, late_y)
        lower = own_half(order, rows, by, i, 1, cores, from_y, late_x)
        outs[i][:half] = upper.astype(jnp.bfloat16)
        outs[i][half:] = lower.astype(jnp.bfloat16)


def stepped(grad, master, moment_one, moment_two):
    one = 0.9 * moment_one + 0.1 * grad
    two = 0.95 * moment_two + 0.05 * grad * grad
    first = 1.0 - 0.9**STEP
    second = 1.0 - 0.95**STEP
    update = one / first / (jnp.sqrt(two / second) + 1e-08)
    return master - 0.002 * (update + 0.1 * master), one, two


def state_body(order, rows, at, flags, ours, soon, later, own_grad, their_grad, from_x, from_y, late_y, late_x, master, moment_one, moment_two, *rest):
    *along_z, state, grad = rest
    cores = (((ours,), own_grad, flags[0:1]), ((soon, later), their_grad, flags[8:9]))
    half = rows // 2
    for lower, near, second in ((0, from_x, late_y), (1, from_y, late_x)):
        total = own_half(order, rows, 0, at, lower, cores, near, second)
        span = pl.ds(lower * half, half)
        for term in along_z:
            total = total + term[span].astype(jnp.float32)
        total = total * flags[16:17]
        grad[span] = total
        for i, value in enumerate(stepped(total, master[span], moment_one[span], moment_two[span])):
            state[i, span] = value.astype(jnp.bfloat16)


def update_body(grad, master, moment_one, moment_two, new_master, new_one, new_two):
    new_master[...], new_one[...], new_two[...] = stepped(
        grad[...], master[...], moment_one[...], moment_two[...]
    )


def piece_columns(planes, rows, by, flip_y, flip_x, flip_c):
    c = lax.axis_index("c")
    block = block_of(planes, -by, flip_y, flip_x)
    return pl.ds(pl.multiple_of((block * 2 + (1 - c if flip_c else c)) * rows, rows), rows)


def normed_at(tokens, span, rstd):
    return (tokens[:, span].astype(jnp.float32) * rstd).astype(jnp.bfloat16)


def each(where, pieces):
    for blocks, piece in zip(where, pieces):
        for k, at in enumerate(blocks):
            yield at, piece.at[k]


def add_keys(planes, rows, where, tokens, rstd, pieces, keys):
    for blocks, piece in zip(where, pieces):
        normed = [normed_at(tokens, piece_columns(planes, rows, *at), rstd) for at in blocks]
        deep = piece[...].reshape(-1, piece.shape[2])
        keys = keys + jnp.dot(
            jnp.concatenate(normed, axis=1), deep, preferred_element_type=jnp.float32
        )
    return keys


def back_of(key_grad, piece):
    return lax.dot_general(
        key_grad[...], piece[...], (((1,), (1,)), ((), ())), preferred_element_type=jnp.float32
    )


def both_ways_body(planes, rows, where, tokens, key_grad, rstd_in, *rest):
    pieces = rest[: len(where)]
    keys_out, input_grad, made, sems = rest[len(where) :]
    features = tokens.shape[1]
    rstd = rstd_in[...]
    keys = jnp.zeros(key_grad.shape, jnp.float32)
    keys = add_keys(planes, rows, where, tokens, rstd, pieces, keys)
    keys_out[...] = keys.astype(jnp.bfloat16)
    inner = jnp.sum(key_grad[...].astype(jnp.float32) * keys, axis=1, keepdims=True) / features
    slope = jnp.broadcast_to(rstd * rstd * inner, (tokens.shape[0], rows))
    found = dict(each(where, pieces))
    copies = []
    for i, (fy, by) in enumerate((fy, by) for fy in (0, 1) for by in range(planes)):
        for at in ((by, fy, fx, fc) for fx in (0, 1) for fc in (0, 1)):
            span = piece_columns(planes, rows, *at)
            back = rstd * back_of(key_grad, found[at])
            made[:, span] = (back - tokens[:, span].astype(jnp.float32) * slope).astype(jnp.bfloat16)
        start = block_of(planes, -by, fy, 0) // 2 * (4 * rows)
        span = pl.ds(pl.multiple_of(start, rows), 4 * rows)
        copies.append(pltpu.make_async_copy(made.at[:, span], input_grad.at[:, span], sems.at[i]))
        copies[-1].start()
    for copy in copies:
        copy.wait()


def quarter_body(rows, weight, out):
    _, _, x, c = place()
    out[...] = weight[pl.ds(pl.multiple_of((x * 2 + c) * rows, rows), rows)]


def stack_body(*refs):
    *parts, out = refs
    for i, part in enumerate(parts):
        out[i] = part[...]


def finish_body(rows, buddy, own, beside, across, diagonal, new_weight, held):
    _, _, x, c = place()
    domain = x * 2 + c
    for flip_x, flip_c, state in ((0, 0, own), (0, 1, beside), (1, 0, across), (1, 1, diagonal)):
        sender = (1 - x if flip_x else x) * 2 + (1 - c if flip_c else c)
        new_weight[pl.ds(pl.multiple_of(sender * rows, rows), rows)] = state[0]

        @pl.when(buddy[sender] == domain)
        def _():
            held[...] = state[...].astype(jnp.float32)


def on_device(tokens, key_grad, weight, master, moment_one, moment_two, live, buddy):
    planes, rows_of, chips, cores = (lax.axis_size(a) for a in ("z", "y", "x", "c"))
    rows, width = master.shape
    many, features = tokens.shape
    if (rows_of, chips, cores) != (2, 2, 2) or rows % 256 or many % 128 or planes < 2 or width != 512:
        return general(tokens, key_grad, weight, master, moment_one, moment_two, live, buddy)
    half = rows // 2
    low, full = jnp.bfloat16, jnp.float32
    live = live.T
    order = sorted(range(1, planes), key=lambda by: min(by, planes - by)) + [0]

    def simple(body, outs, *operands, limit=12, **more):
        return local(body, outs, 8, 8, limit, *operands, **more)

    quarter, = simple(lambda *refs: quarter_body(rows, *refs), [((rows, width), low)], weight)
    opposite = lax.ppermute(quarter, ("y", "x"), [(0, 3), (1, 2), (2, 1), (3, 0)])
    quarters, opposites = [quarter], [opposite]
    for by in range(1, planes):
        quarters.append(shift(quarters[-1], "z", 1))
        opposites.append(shift(opposites[-1], "z", 1))
    column, = simple(
        stack_body,
        [((planes, rows, width), low)],
        *quarters,
    )
    corner, = simple(stack_body, [((planes, rows, width), low)], *opposites)

    ours, soon, later, rstd = prepare(tokens, rows, order)
    flags, = simple(
        lambda *refs: flags_body(many, *refs),
        [((24, width), full)],
        after(live, soon),
        scalars=1,
    )
    grads = key_grad, shift(after(key_grad, soon), "c", 1)
    theirs = shift(soon, "c", 1), shift(after(later, grads[1]), "c", 1)
    cores = (flags, ours, *theirs, *grads)

    groups = order[: planes // 2], order[planes // 2 :]
    came = []
    for group, part in zip(groups, theirs):
        to_x, to_y = simple(
            lambda *refs: first_body(order, rows, group, *refs),
            [((2, len(group), half, width), low)] * 2,
            flags, ours, part, *grads,
        )
        came.append((shift(to_x, "x", 1), shift(to_y, "y", 1)))
    late = []
    along_z = []
    first_out = ()
    for group, (from_x, from_y), ties in zip(groups, came, ((), quarters[1:3])):
        to_y, to_x = simple(
            lambda *refs: second_body(order, rows, group, *refs),
            [((len(group), half, width), low)] * 2,
            *cores, after(from_x, *(late_out if along_z else ())), after(from_y, *ties),
        )
        late_out = (to_y, to_x)
        late.append((shift(to_y, "y", 1), shift(to_x, "x", 1)))
        sent = [by for by in group if by]
        to_z = simple(
            lambda *refs: third_body(order, rows, sent, *refs),
            [((rows, width), low)] * len(sent),
            *cores, from_x, from_y, after(late[-1][0], *(first_out or (*quarters[3:], opposites[1]))), late[-1][1],
        )
        first_out = to_z
        along_z += [shift(term, "z", by) for by, term in zip(sent, to_z)]
    column_late = after(column, *late[1], *to_z, opposites[2])
    over_x, over_y = shift(column_late, "x", 1), shift(column_late, "y", 1)
    along_z[0] = after(along_z[0], corner)
    state, grad = simple(
        lambda *refs: state_body(order, rows, len(groups[1]) - 1, *refs),
        [((3, rows, width), low), ((rows, width), full)],
        *cores, *came[1], *late[1], master, moment_one, moment_two, *along_z,
    )

    pieces, where = [], []
    for fy, fx, piece in ((0, 0, column), (1, 1, corner), (0, 1, over_x), (1, 0, over_y)):
        pieces += [piece, shift(piece, "c", 1)]
        where += [[(by, fy, fx, fc) for by in range(planes)] for fc in (0, 1)]
    keys, input_grad = pl.pallas_call(
        lambda *refs: both_ways_body(planes, rows, where, *refs),
        out_shape=[
            jax.ShapeDtypeStruct((many, width), low),
            jax.ShapeDtypeStruct((many, features), low),
        ],
        in_specs=[VMEM] * (3 + len(pieces)),
        out_specs=[VMEM, pl.BlockSpec(memory_space=pltpu.HBM)],
        scratch_shapes=[
            pltpu.VMEM((many, features), low),
            pltpu.SemaphoreType.DMA((2 * planes,)),
        ],
        cost_estimate=pl.CostEstimate(flops=8, bytes_accessed=8, transcendentals=0),
        compiler_params=pltpu.CompilerParams(vmem_limit_bytes=24 * MIB),
    )(tokens, key_grad, rstd, *pieces)

    beside = shift(state, "c", 1)
    across = shift(after(state, beside), "x", 1)
    new_master, new_one, new_two = simple(
        update_body, [((rows, width), full)] * 3, grad, master, moment_one, moment_two
    )
    diagonal = shift(after(across, keys, new_one), "c", 1)
    new_weight, held = simple(
        lambda *refs: finish_body(rows, *refs),
        [(weight.shape, low), ((3, rows, width), full)],
        buddy, state, beside, across, diagonal,
        scalars=1,
    )
    return (keys, input_grad, new_weight, new_master, new_one, new_two, held)


def solution(mesh):
    members, domains = mesh.devices.shape
    split = Mesh(mesh.devices.reshape(members // 2, 2, domains // 2, 2), ("z", "y", "x", "c"))
    every = ("z", "y", "x", "c")
    placed = (
        P(every, None),
        P(every, None),
        P(("z", "y"), None),
        P(every, None),
        P(every, None),
        P(every, None),
        P(),
        P(),
    )
    return jax.shard_map(
        on_device,
        mesh=split,
        in_specs=placed,
        out_specs=(
            P(every, None),
            P(every, None),
            P(("z", "y"), None),
            P(every, None),
            P(every, None),
            P(every, None),
            P(None, every, None),
        ),
        check_vma=False,
    )
```

time: 548 us -> 109 us (0.20)
  waiting for transfers between devices: 488 us -> 60.6 us
  starting transfers between devices: 0.2 us -> 29.4 us
  matrix products: 24.2 us -> 0 us
  Pallas kernels: 0 us -> 18.4 us
  between operations: 17.2 us -> 0.81 us
  other arithmetic: 12.4 us -> 0 us
  local copies, waits for them, and re-layouts: 5.56 us -> 0.03 us
    reduce_scatter x2 -> x0, waiting for transfers between devices: 318 us -> none  [the longest x1 285 us: on_device(): lax.psum_scatter(product * scale, 'fsdp', scatter_dimension=0, tiled=True)]
    all_gather x3 -> x0, waiting for transfers between devices: 169 us -> none  [the longest x1 121 us: on_device(): whole = lax.all_gather(weight, 'fsdp', axis=0, tiled=True)]
    ppermute x0 -> x30, waiting for transfers between devices: none -> 60.6 us  [the longest x29 57.6 us: shift(): lax.ppermute(value, axis, [(i, (i + by) % size) for i in range(size)])]
    ppermute x0 -> x30, starting transfers between devices: none -> 29.4 us  [the longest x29 25.8 us: shift(): lax.ppermute(value, axis, [(i, (i + by) % size) for i in range(size)])]
    dot_general x3 -> x0, matrix products: 24.2 us -> none  [the longest x1 10.4 us: on_device(): lax.dot_general(normed, key_grad, (((0,), (0,)), ((), ())), preferred_ele...]
    pallas_call x0 -> x15, Pallas kernels: none -> 18.4 us  [the longest x13 8.74 us: local(): pl.pallas_call(body, out_shape=[jax.ShapeDtypeStruct(s, t) for s, t in ou...]
    convert_element_type x3 -> x0, other arithmetic: 5.96 us -> none  [the longest x1 3.11 us: on_device(): (rstd * (back - hat * jnp.mean(back * hat, axis=1, keepdims=True))).astyp...]
  transfers between devices with their start and end apart: 5 -> 30, of which waited for: 4 -> 19; matrix products, arithmetic and copies ran while one was open for 4% -> 0% of each run, Pallas kernels for 0% -> 12%
where the time goes in v1:
time: 109 us
  waiting for transfers between devices  60.6 us (56%)
  starting transfers between devices  29.4 us (27%)
  Pallas kernels  18.4 us (17%)
    ppermute x29, waiting for transfers between devices, shift(): lax.ppermute(value, axis, [(i, (i + by) % size) for i in range(size)])  57.6 us
    ppermute x29, starting transfers between devices, shift(): lax.ppermute(value, axis, [(i, (i + by) % size) for i in range(size)])  25.8 us
    pallas_call x13, Pallas kernels, local(): pl.pallas_call(body, out_shape=[jax.ShapeDtypeStruct(s, t) for s, t in ou...  8.74 us
    pallas_call x1, Pallas kernels, on_device(): pl.pallas_call(lambda *refs: both_ways_body(planes, rows, where, *refs),...  6.42 us
    ppermute x1, starting transfers between devices, on_device(): lax.ppermute(quarter, ('y', 'x'), [(0, 3), (1, 2), (2, 1), (3, 0)])  3.66 us
    pallas_call x1, Pallas kernels, prepare(): pl.pallas_call(lambda *refs: prepare_body(rows, order, *refs), out_shape=...  3.27 us
    ppermute x1, waiting for transfers between devices, on_device(): lax.ppermute(quarter, ('y', 'x'), [(0, 3), (1, 2), (2, 1), (3, 0)])  3.04 us
  transfers between devices with their start and end apart: 30, of which 19 were waited for; matrix products, arithmetic and copies ran while one was open for 0% of the time, Pallas kernels for 12%

profile of v1, /device:TPU:0, one launch (start us, length us, event | category | flops | bytes accessed | tf_op | source)
XLA Modules:
  0.0 109.3 jit_solution(9338688889722159476)
XLA Ops:
  0.7 3.3 %shard_map.135 = (bf16[256,4096]{1,0:T(8,128)(2,1)S(1)}, bf16[256,2048]{1,0:T(8,128)(2,1)S(1)}, bf16[256,2048]{1,0:T(8,128)(2,1)S(1)}, f32[256,1]{1,0:T(8,128)S(1)}) custom-call(bf16[256,8192]{1,0:T(8,128)(2,1)} %refs_0_.6), custom_call_target="tpu_custom_call" | custom-call | flops 8 | bytes 8 | tf_op jit(solution)/shard_map/pallas_call | solution.py:183
  3.9 0.5 collective-permute-start.10
  4.5 0.1 collective-permute-start.9
  4.5 1.1 collective-permute-done.10.refs_4_.refs_5_
  5.6 0.4 collective-permute-start.11
  6.0 3.7 %collective-permute-start.4 = (bf16[256,512]{1,0:T(8,128)(2,1)S(1)}, bf16[256,512]{1,0:T(8,128)(2,1)S(1)}, u32[]{:S(2)}, u32[]{:S(2)}) collective-permute-start(bf16[256,512]{1,0:T(8,128)(2,1)S(1)} %shard_map.136.refs_0_), channel_id=1, source_target_pairs={{0,6},{2,4},{4,2},{6,0},{1,7},{3,5},{5,3},{7,1},{8,14},{10,12},{12... | collective-permute-start | bytes 786440 | tf_op jit(solution)/shard_map/ppermute | solution.py:378
  9.7 1.6 %collective-permute-start = (bf16[256,512]{1,0:T(8,128)(2,1)S(1)}, bf16[256,512]{1,0:T(8,128)(2,1)S(1)}, u32[]{:S(2)}, u32[]{:S(2)}) collective-permute-start(bf16[256,512]{1,0:T(8,128)(2,1)S(1)} %shard_map.136.refs_0_), channel_id=1, source_target_pairs={{0,8},{8,16},{16,24},{24,0},{1,9},{9,17},{17,25},{25,1},{2,10},{10... | collective-permute-start | bytes 786440 | tf_op jit(solution)/shard_map/ppermute | solution.py:14
  11.3 0.6 shard_map.139.refs_0_
  11.9 0.8 shard_map.141
  12.7 0.6 collective-permute-start.13
  13.3 0.5 collective-permute-start.14
  13.8 3.0 %collective-permute-done.4.refs_0_ = bf16[256,512]{1,0:T(8,128)(2,1)S(1)} collective-permute-done((bf16[256,512]{1,0:T(8,128)(2,1)S(1)}, bf16[256,512]{1,0:T(8,128)(2,1)S(1)}, u32[]{:S(2)}, u32[]{:S(2)}) %collective-permute-start.4) | collective-permute-done | bytes 262176 | tf_op jit(solution)/shard_map/ppermute | solution.py:378
  16.8 2.0 %collective-permute-start.5 = (bf16[256,512]{1,0:T(8,128)(2,1)S(1)}, bf16[256,512]{1,0:T(8,128)(2,1)S(1)}, u32[]{:S(2)}, u32[]{:S(2)}) collective-permute-start(bf16[256,512]{1,0:T(8,128)(2,1)S(1)} %collective-permute-done.4.refs_0_), channel_id=1, source_target_pairs={{0,8},{8,16},{16,24},{24,0},{1,9},{9,17},{17,25},{25,1},{2,10},{10... | collective-permute-start | bytes 786440 | tf_op jit(solution)/shard_map/ppermute | solution.py:14
  18.8 0.8 shard_map.140
  19.6 1.6 %collective-permute-start.15 = (bf16[2,2,128,512]{3,2,1,0:T(8,128)(2,1)S(1)}, bf16[2,2,128,512]{3,2,1,0:T(8,128)(2,1)S(1)}, u32[]{:S(2)}, u32[]{:S(2)}) collective-permute-start(bf16[2,2,128,512]{3,2,1,0:T(8,128)(2,1)S(1)} %get-tuple-element.54), channel_id=1, source_target_pairs={{0,4},{4,0},{1,5},{5,1},{2,6},{6,2},{3,7},{7,3},{8,12},{12,8},{9,1... | collective-permute-start | bytes 1572872 | tf_op jit(solution)/shard_map/ppermute | solution.py:14
  21.2 0.0 collective-permute-done.refs_1_
  21.2 1.5 %collective-permute-start.12 = (bf16[2,2,128,512]{3,2,1,0:T(8,128)(2,1)S(1)}, bf16[2,2,128,512]{3,2,1,0:T(8,128)(2,1)S(1)}, u32[]{:S(2)}, u32[]{:S(2)}) collective-permute-start(bf16[2,2,128,512]{3,2,1,0:T(8,128)(2,1)S(1)} %get-tuple-element.48), channel_id=1, source_target_pairs={{0,2},{2,0},{1,3},{3,1},{4,6},{6,4},{5,7},{7,5},{8,10},{10,8},{9,1... | collective-permute-start | bytes 1572872 | tf_op jit(solution)/shard_map/ppermute | solution.py:14
  22.7 3.6 %collective-permute-done.5.refs_1_ = bf16[256,512]{1,0:T(8,128)(2,1)S(1)} collective-permute-done((bf16[256,512]{1,0:T(8,128)(2,1)S(1)}, bf16[256,512]{1,0:T(8,128)(2,1)S(1)}, u32[]{:S(2)}, u32[]{:S(2)}) %collective-permute-start.5) | collective-permute-done | bytes 262176 | tf_op jit(solution)/shard_map/ppermute | solution.py:14
  26.4 0.0 collective-permute-start.1
  26.4 2.2 %collective-permute-done.13.refs_6_ = bf16[2,2,128,512]{3,2,1,0:T(8,128)(2,1)S(1)} collective-permute-done((bf16[2,2,128,512]{3,2,1,0:T(8,128)(2,1)S(1)}, bf16[2,2,128,512]{3,2,1,0:T(8,128)(2,1)S(1)}, u32[]{:S(2)}, u32[]{:S(2)}) %collective-permute-start.13) | collective-permute-done | bytes 524320 | tf_op jit(solution)/shard_map/ppermute | solution.py:14
  28.6 1.6 %collective-permute-start.6 = (bf16[256,512]{1,0:T(8,128)(2,1)S(1)}, bf16[256,512]{1,0:T(8,128)(2,1)S(1)}, u32[]{:S(2)}, u32[]{:S(2)}) collective-permute-start(bf16[256,512]{1,0:T(8,128)(2,1)S(1)} %collective-permute-done.5.refs_1_), channel_id=1, source_target_pairs={{0,8},{8,16},{16,24},{24,0},{1,9},{9,17},{17,25},{25,1},{2,10},{10... | collective-permute-start | bytes 786440 | tf_op jit(solution)/shard_map/ppermute | solution.py:14
  30.2 7.3 %collective-permute-done.1.refs_2_ = bf16[256,512]{1,0:T(8,128)(2,1)S(1)} collective-permute-done((bf16[256,512]{1,0:T(8,128)(2,1)S(1)}, bf16[256,512]{1,0:T(8,128)(2,1)S(1)}, u32[]{:S(2)}, u32[]{:S(2)}) %collective-permute-start.1) | collective-permute-done | bytes 262176 | tf_op jit(solution)/shard_map/ppermute | solution.py:14
  37.4 0.5 shard_map.142
  37.9 1.6 %collective-permute-start.18 = (bf16[2,128,512]{2,1,0:T(8,128)(2,1)S(1)}, bf16[2,128,512]{2,1,0:T(8,128)(2,1)S(1)}, u32[]{:S(2)}, u32[]{:S(2)}) collective-permute-start(bf16[2,128,512]{2,1,0:T(8,128)(2,1)S(1)} %get-tuple-element.51), channel_id=1, source_target_pairs={{0,4},{4,0},{1,5},{5,1},{2,6},{6,2},{3,7},{7,3},{8,12},{12,8},{9,1... | collective-permute-start | bytes 786440 | tf_op jit(solution)/shard_map/ppermute | solution.py:14
  39.5 0.0 collective-permute-done.15.refs_7_
  39.5 1.5 %collective-permute-start.19 = (bf16[2,128,512]{2,1,0:T(8,128)(2,1)S(1)}, bf16[2,128,512]{2,1,0:T(8,128)(2,1)S(1)}, u32[]{:S(2)}, u32[]{:S(2)}) collective-permute-start(bf16[2,128,512]{2,1,0:T(8,128)(2,1)S(1)} %get-tuple-element.52), channel_id=1, source_target_pairs={{0,2},{2,0},{1,3},{3,1},{4,6},{6,4},{5,7},{7,5},{8,10},{10,8},{9,1... | collective-permute-start | bytes 786440 | tf_op jit(solution)/shard_map/ppermute | solution.py:14
  41.0 0.5 shard_map.143
  41.5 1.3 %collective-permute-start.16 = (bf16[2,128,512]{2,1,0:T(8,128)(2,1)S(1)}, bf16[2,128,512]{2,1,0:T(8,128)(2,1)S(1)}, u32[]{:S(2)}, u32[]{:S(2)}) collective-permute-start(bf16[2,128,512]{2,1,0:T(8,128)(2,1)S(1)} %get-tuple-element.56), channel_id=1, source_target_pairs={{0,4},{4,0},{1,5},{5,1},{2,6},{6,2},{3,7},{7,3},{8,12},{12,8},{9,1... | collective-permute-start | bytes 786440 | tf_op jit(solution)/shard_map/ppermute | solution.py:14
  42.9 0.2 collective-permute-done.6.refs_2_
  43.0 1.2 %collective-permute-start.17 = (bf16[2,128,512]{2,1,0:T(8,128)(2,1)S(1)}, bf16[2,128,512]{2,1,0:T(8,128)(2,1)S(1)}, u32[]{:S(2)}, u32[]{:S(2)}) collective-permute-start(bf16[2,128,512]{2,1,0:T(8,128)(2,1)S(1)} %get-tuple-element.57), channel_id=1, source_target_pairs={{0,2},{2,0},{1,3},{3,1},{4,6},{6,4},{5,7},{7,5},{8,10},{10,8},{9,1... | collective-permute-start | bytes 786440 | tf_op jit(solution)/shard_map/ppermute | solution.py:14
  44.2 1.8 %collective-permute-done.2.refs_3_ = bf16[256,512]{1,0:T(8,128)(2,1)S(1)} collective-permute-done((bf16[256,512]{1,0:T(8,128)(2,1)S(1)}, bf16[256,512]{1,0:T(8,128)(2,1)S(1)}, u32[]{:S(2)}, u32[]{:S(2)}) %collective-permute-start.2) | collective-permute-done | bytes 262176 | tf_op jit(solution)/shard_map/ppermute | solution.py:14
  46.0 0.1 shard_map.137.refs_3_
  46.1 0.0 collective-permute-done.18.refs_8_
  46.1 2.7 %collective-permute-done.19.refs_9_ = bf16[2,128,512]{2,1,0:T(8,128)(2,1)S(1)} collective-permute-done((bf16[2,128,512]{2,1,0:T(8,128)(2,1)S(1)}, bf16[2,128,512]{2,1,0:T(8,128)(2,1)S(1)}, u32[]{:S(2)}, u32[]{:S(2)}) %collective-permute-start.19) | collective-permute-done | bytes 262176 | tf_op jit(solution)/shard_map/ppermute | solution.py:14
  48.8 0.6 shard_map.144
  49.3 0.9 collective-permute-done.16.refs_8_
  50.2 2.4 %collective-permute-done.17.refs_9_ = bf16[2,128,512]{2,1,0:T(8,128)(2,1)S(1)} collective-permute-done((bf16[2,128,512]{2,1,0:T(8,128)(2,1)S(1)}, bf16[2,128,512]{2,1,0:T(8,128)(2,1)S(1)}, u32[]{:S(2)}, u32[]{:S(2)}) %collective-permute-start.17) | collective-permute-done | bytes 262176 | tf_op jit(solution)/shard_map/ppermute | solution.py:14
  52.6 0.4 shard_map.145
  53.0 2.0 %collective-permute-start.22 = (bf16[4,256,512]{2,1,0:T(8,128)(2,1)S(1)}, bf16[4,256,512]{2,1,0:T(8,128)(2,1)S(1)}, u32[]{:S(2)}, u32[]{:S(2)}) collective-permute-start(bf16[4,256,512]{2,1,0:T(8,128)(2,1)S(1)} %shard_map.137.refs_3_), channel_id=1, source_target_pairs={{0,4},{4,0},{1,5},{5,1},{2,6},{6,2},{3,7},{7,3},{8,12},{12,8},{9,1... | collective-permute-start | bytes 3145736 | tf_op jit(solution)/shard_map/ppermute | solution.py:14
  55.0 1.5 %collective-permute-start.20 = (bf16[4,256,512]{2,1,0:T(8,128)(2,1)S(1)}, bf16[4,256,512]{2,1,0:T(8,128)(2,1)S(1)}, u32[]{:S(2)}, u32[]{:S(2)}) collective-permute-start(bf16[4,256,512]{2,1,0:T(8,128)(2,1)S(1)} %shard_map.137.refs_3_), channel_id=1, source_target_pairs={{0,2},{2,0},{1,3},{3,1},{4,6},{6,4},{5,7},{7,5},{8,10},{10,8},{9,1... | collective-permute-start | bytes 3145736 | tf_op jit(solution)/shard_map/ppermute | solution.py:14
  56.5 1.6 %collective-permute-start.24 = (bf16[256,512]{1,0:T(8,128)(2,1)S(1)}, bf16[256,512]{1,0:T(8,128)(2,1)S(1)}, u32[]{:S(2)}, u32[]{:S(2)}) collective-permute-start(bf16[256,512]{1,0:T(8,128)(2,1)S(1)} %get-tuple-element.59), channel_id=1, source_target_pairs={{0,8},{8,16},{16,24},{24,0},{1,9},{9,17},{17,25},{25,1},{2,10},{10... | collective-permute-start | bytes 786440 | tf_op jit(solution)/shard_map/ppermute | solution.py:14
  58.1 2.2 %collective-permute-start.25 = (bf16[256,512]{1,0:T(8,128)(2,1)S(1)}, bf16[256,512]{1,0:T(8,128)(2,1)S(1)}, u32[]{:S(2)}, u32[]{:S(2)}) collective-permute-start(bf16[256,512]{1,0:T(8,128)(2,1)S(1)} %get-tuple-element.60), channel_id=1, source_target_pairs={{0,24},{8,0},{16,8},{24,16},{1,25},{9,1},{17,9},{25,17},{2,26},{10... | collective-permute-start | bytes 786440 | tf_op jit(solution)/shard_map/ppermute | solution.py:14
  60.3 0.8 collective-permute-start.26
  61.1 0.1 shard_map.138.refs_5_
  61.2 0.0 copy-start.1
  61.2 6.3 %collective-permute-done.24.refs_13_ = bf16[256,512]{1,0:T(8,128)(2,1)S(1)} collective-permute-done((bf16[256,512]{1,0:T(8,128)(2,1)S(1)}, bf16[256,512]{1,0:T(8,128)(2,1)S(1)}, u32[]{:S(2)}, u32[]{:S(2)}) %collective-permute-start.24) | collective-permute-done | bytes 262176 | tf_op jit(solution)/shard_map/ppermute | solution.py:14
  67.5 3.0 %collective-permute-done.25.refs_14_ = bf16[256,512]{1,0:T(8,128)(2,1)S(1)} collective-permute-done((bf16[256,512]{1,0:T(8,128)(2,1)S(1)}, bf16[256,512]{1,0:T(8,128)(2,1)S(1)}, u32[]{:S(2)}, u32[]{:S(2)}) %collective-permute-start.25) | collective-permute-done | bytes 262176 | tf_op jit(solution)/shard_map/ppermute | solution.py:14
  70.5 11.4 %collective-permute-done.26.refs_15_ = bf16[256,512]{1,0:T(8,128)(2,1)S(1)} collective-permute-done((bf16[256,512]{1,0:T(8,128)(2,1)S(1)}, bf16[256,512]{1,0:T(8,128)(2,1)S(1)}, u32[]{:S(2)}, u32[]{:S(2)}) %collective-permute-start.26) | collective-permute-done | bytes 262176 | tf_op jit(solution)/shard_map/ppermute | solution.py:14
  81.9 0.9 shard_map.147
  82.8 0.1 collective-permute-start.27
  82.9 0.5 collective-permute-start.3
  83.4 0.1 collective-permute-start.8
  83.5 0.4 collective-permute-start.23
  83.9 0.1 collective-permute-start.21
  84.0 1.2 %collective-permute-done.27.refs_2_ = bf16[3,256,512]{2,1,0:T(8,128)(2,1)S(1)} collective-permute-done((bf16[3,256,512]{2,1,0:T(8,128)(2,1)S(1)}, bf16[3,256,512]{2,1,0:T(8,128)(2,1)S(1)}, u32[]{:S(2)}, u32[]{:S(2)}) %collective-permute-start.27) | collective-permute-done | bytes 786464 | tf_op jit(solution)/shard_map/ppermute | solution.py:14
  85.2 0.5 collective-permute-start.28
  85.7 1.4 %shard_map.148 = (f32[256,512]{1,0:T(8,128)}, f32[256,512]{1,0:T(8,128)}, f32[256,512]{1,0:T(8,128)}) custom-call(f32[256,512]{1,0:T(8,128)S(1)} %get-tuple-element.68.grad, f32[256,512]{1,0:T(8,128)S(1)} %copy-done.2, f32[256,512]{1,0:T(8,128)S(1)} %copy-done.3, f32[256,512]{1,0:T(8,128)S(1)} %copy-done.4), custom_call_target="tpu_custom_call" | custom-call | flops 8 | bytes 8 | tf_op jit(solution)/shard_map/pallas_call | solution.py:115
  87.1 1.1 %collective-permute-done.8.refs_6_ = bf16[4,256,512]{2,1,0:T(8,128)(2,1)S(1)} collective-permute-done((bf16[4,256,512]{2,1,0:T(8,128)(2,1)S(1)}, bf16[4,256,512]{2,1,0:T(8,128)(2,1)S(1)}, u32[]{:S(2)}, u32[]{:S(2)}) %collective-permute-start.8) | collective-permute-done | bytes 1048608 | tf_op jit(solution)/shard_map/ppermute | solution.py:14
  88.2 1.5 %collective-permute-done.23.refs_10_ = bf16[4,256,512]{2,1,0:T(8,128)(2,1)S(1)} collective-permute-done((bf16[4,256,512]{2,1,0:T(8,128)(2,1)S(1)}, bf16[4,256,512]{2,1,0:T(8,128)(2,1)S(1)}, u32[]{:S(2)}, u32[]{:S(2)}) %collective-permute-start.23) | collective-permute-done | bytes 1048608 | tf_op jit(solution)/shard_map/ppermute | solution.py:14
  89.7 1.5 %collective-permute-done.21.refs_8_ = bf16[4,256,512]{2,1,0:T(8,128)(2,1)S(1)} collective-permute-done((bf16[4,256,512]{2,1,0:T(8,128)(2,1)S(1)}, bf16[4,256,512]{2,1,0:T(8,128)(2,1)S(1)}, u32[]{:S(2)}, u32[]{:S(2)}) %collective-permute-start.21) | collective-permute-done | bytes 1048608 | tf_op jit(solution)/shard_map/ppermute | solution.py:14
  91.2 6.4 %shard_map.146 = (bf16[256,512]{1,0:T(8,128)(2,1)}, bf16[256,8192]{1,0:T(8,128)(2,1)}) custom-call(bf16[256,8192]{1,0:T(8,128)(2,1)S(1)} %copy-done.1, bf16[256,512]{1,0:T(8,128)(2,1)S(1)} %copy-done, f32[256,1]{1,0:T(8,128)S(1)} %get-tuple-element.41.refs_2_, bf16[4,256,512]{2,1,0:T(8,128)(2,1)S(1)} %shard_map.137.refs_3_, ...), custom_call_target="tpu_custom_call" | custom-call | flops 8 | bytes 8 | tf_op jit(solution)/shard_map/pallas_call | solution.py:442
  97.6 7.2 %collective-permute-done.28.refs_3_ = bf16[3,256,512]{2,1,0:T(8,128)(2,1)S(1)} collective-permute-done((bf16[3,256,512]{2,1,0:T(8,128)(2,1)S(1)}, bf16[3,256,512]{2,1,0:T(8,128)(2,1)S(1)}, u32[]{:S(2)}, u32[]{:S(2)}) %collective-permute-start.28) | collective-permute-done | bytes 786464 | tf_op jit(solution)/shard_map/ppermute | solution.py:14
  104.8 2.3 %collective-permute-done.29.refs_4_ = bf16[3,256,512]{2,1,0:T(8,128)(2,1)S(1)} collective-permute-done((bf16[3,256,512]{2,1,0:T(8,128)(2,1)S(1)}, bf16[3,256,512]{2,1,0:T(8,128)(2,1)S(1)}, u32[]{:S(2)}, u32[]{:S(2)}) %collective-permute-start.29) | collective-permute-done | bytes 786464 | tf_op jit(solution)/shard_map/ppermute | solution.py:14
  107.1 2.2 %shard_map.149 = (bf16[1024,512]{1,0:T(8,128)(2,1)}, f32[3,256,512]{2,1,0:T(8,128)}) custom-call(s32[4]{0:T(128)S(1)} %copy-done.7, bf16[3,256,512]{2,1,0:T(8,128)(2,1)S(1)} %get-tuple-element.67.refs_1_, bf16[3,256,512]{2,1,0:T(8,128)(2,1)S(1)} %collective-permute-done.27.refs_2_, bf16[3,256,512]{2,1,0:T(8,128)(2,1)S(1)} %collective-permute-done.28.refs_3_, ...), custom_call_target="tpu_custom_call" | custom-call | flops 8 | bytes 8 | tf_op jit(solution)/shard_map/pallas_call | solution.py:115
  (27 shorter events, 0.1 us)
Async XLA Ops:
  0.6 3.3 %copy-start = (bf16[256,512]{1,0:T(8,128)(2,1)S(1)}, bf16[256,512]{1,0:T(8,128)(2,1)}, u32[]{:S(2)}) copy-start(bf16[256,512]{1,0:T(8,128)(2,1)} %refs_4_.9) | copy-start | bytes 786436
  0.6 5.4 %copy-start.5 = (bf16[1024,512]{1,0:T(8,128)(2,1)S(1)}, bf16[1024,512]{1,0:T(8,128)(2,1)}, u32[]{:S(2)}) copy-start(bf16[1024,512]{1,0:T(8,128)(2,1)} %refs_0_.5) | copy-start | bytes 3145732
  0.7 10.6 %copy-start.6 = (s32[8,4]{0,1:T(4,128)S(1)}, s32[8,4]{0,1:T(4,128)}, u32[]{:S(2)}) copy-start(s32[8,4]{0,1:T(4,128)} %param.14) | copy-start | bytes 388
  3.9 1.7 %collective-permute-start.10 = (bf16[256,512]{1,0:T(8,128)(2,1)S(1)}, bf16[256,512]{1,0:T(8,128)(2,1)S(1)}, u32[]{:S(2)}, u32[]{:S(2)}) collective-permute-start(bf16[256,512]{1,0:T(8,128)(2,1)S(1)} %copy-done), channel_id=1, source_target_pairs={{0,1},{1,0},{2,3},{3,2},{4,5},{5,4},{6,7},{7,6},{8,9},{9,8},{10,11... | collective-permute-start | bytes 786440 | tf_op jit(solution)/shard_map/ppermute | solution.py:14
  4.5 7.4 %collective-permute-start.9 = (bf16[256,2048]{1,0:T(8,128)(2,1)S(1)}, bf16[256,2048]{1,0:T(8,128)(2,1)S(1)}, u32[]{:S(2)}, u32[]{:S(2)}) collective-permute-start(bf16[256,2048]{1,0:T(8,128)(2,1)S(1)} %get-tuple-element.42), channel_id=1, source_target_pairs={{0,1},{1,0},{2,3},{3,2},{4,5},{5,4},{6,7},{7,6},{8,9},{9,8},{10,11... | collective-permute-start | bytes 3145736 | tf_op jit(solution)/shard_map/ppermute | solution.py:14
  5.6 13.2 %collective-permute-start.11 = (bf16[256,2048]{1,0:T(8,128)(2,1)S(1)}, bf16[256,2048]{1,0:T(8,128)(2,1)S(1)}, u32[]{:S(2)}, u32[]{:S(2)}) collective-permute-start(bf16[256,2048]{1,0:T(8,128)(2,1)S(1)} %get-tuple-element.47), channel_id=1, source_target_pairs={{0,1},{1,0},{2,3},{3,2},{4,5},{5,4},{6,7},{7,6},{8,9},{9,8},{10,11... | collective-permute-start | bytes 3145736 | tf_op jit(solution)/shard_map/ppermute | solution.py:14
  6.0 10.8 %collective-permute-start.4 = (bf16[256,512]{1,0:T(8,128)(2,1)S(1)}, bf16[256,512]{1,0:T(8,128)(2,1)S(1)}, u32[]{:S(2)}, u32[]{:S(2)}) collective-permute-start(bf16[256,512]{1,0:T(8,128)(2,1)S(1)} %shard_map.136.refs_0_), channel_id=1, source_target_pairs={{0,6},{2,4},{4,2},{6,0},{1,7},{3,5},{5,3},{7,1},{8,14},{10,12},{12... | collective-permute-start | bytes 786440 | tf_op jit(solution)/shard_map/ppermute | solution.py:378
  9.7 11.6 %collective-permute-start = (bf16[256,512]{1,0:T(8,128)(2,1)S(1)}, bf16[256,512]{1,0:T(8,128)(2,1)S(1)}, u32[]{:S(2)}, u32[]{:S(2)}) collective-permute-start(bf16[256,512]{1,0:T(8,128)(2,1)S(1)} %shard_map.136.refs_0_), channel_id=1, source_target_pairs={{0,8},{8,16},{16,24},{24,0},{1,9},{9,17},{17,25},{25,1},{2,10},{10... | collective-permute-start | bytes 786440 | tf_op jit(solution)/shard_map/ppermute | solution.py:14
  12.7 15.9 %collective-permute-start.13 = (bf16[2,2,128,512]{3,2,1,0:T(8,128)(2,1)S(1)}, bf16[2,2,128,512]{3,2,1,0:T(8,128)(2,1)S(1)}, u32[]{:S(2)}, u32[]{:S(2)}) collective-permute-start(bf16[2,2,128,512]{3,2,1,0:T(8,128)(2,1)S(1)} %get-tuple-element.49), channel_id=1, source_target_pairs={{0,2},{2,0},{1,3},{3,1},{4,6},{6,4},{5,7},{7,5},{8,10},{10,8},{9,1... | collective-permute-start | bytes 1572872 | tf_op jit(solution)/shard_map/ppermute | solution.py:14
  13.3 16.9 %collective-permute-start.14 = (bf16[2,2,128,512]{3,2,1,0:T(8,128)(2,1)S(1)}, bf16[2,2,128,512]{3,2,1,0:T(8,128)(2,1)S(1)}, u32[]{:S(2)}, u32[]{:S(2)}) collective-permute-start(bf16[2,2,128,512]{3,2,1,0:T(8,128)(2,1)S(1)} %get-tuple-element.50), channel_id=1, source_target_pairs={{0,4},{4,0},{1,5},{5,1},{2,6},{6,2},{3,7},{7,3},{8,12},{12,8},{9,1... | collective-permute-start | bytes 1572872 | tf_op jit(solution)/shard_map/ppermute | solution.py:14
  16.8 9.5 %collective-permute-start.5 = (bf16[256,512]{1,0:T(8,128)(2,1)S(1)}, bf16[256,512]{1,0:T(8,128)(2,1)S(1)}, u32[]{:S(2)}, u32[]{:S(2)}) collective-permute-start(bf16[256,512]{1,0:T(8,128)(2,1)S(1)} %collective-permute-done.4.refs_0_), channel_id=1, source_target_pairs={{0,8},{8,16},{16,24},{24,0},{1,9},{9,17},{17,25},{25,1},{2,10},{10... | collective-permute-start | bytes 786440 | tf_op jit(solution)/shard_map/ppermute | solution.py:14
  19.6 19.9 %collective-permute-start.15 = (bf16[2,2,128,512]{3,2,1,0:T(8,128)(2,1)S(1)}, bf16[2,2,128,512]{3,2,1,0:T(8,128)(2,1)S(1)}, u32[]{:S(2)}, u32[]{:S(2)}) collective-permute-start(bf16[2,2,128,512]{3,2,1,0:T(8,128)(2,1)S(1)} %get-tuple-element.54), channel_id=1, source_target_pairs={{0,4},{4,0},{1,5},{5,1},{2,6},{6,2},{3,7},{7,3},{8,12},{12,8},{9,1... | collective-permute-start | bytes 1572872 | tf_op jit(solution)/shard_map/ppermute | solution.py:14
  21.2 19.8 %collective-permute-start.12 = (bf16[2,2,128,512]{3,2,1,0:T(8,128)(2,1)S(1)}, bf16[2,2,128,512]{3,2,1,0:T(8,128)(2,1)S(1)}, u32[]{:S(2)}, u32[]{:S(2)}) collective-permute-start(bf16[2,2,128,512]{3,2,1,0:T(8,128)(2,1)S(1)} %get-tuple-element.48), channel_id=1, source_target_pairs={{0,2},{2,0},{1,3},{3,1},{4,6},{6,4},{5,7},{7,5},{8,10},{10,8},{9,1... | collective-permute-start | bytes 1572872 | tf_op jit(solution)/shard_map/ppermute | solution.py:14
  26.4 11.0 %collective-permute-start.1 = (bf16[256,512]{1,0:T(8,128)(2,1)S(1)}, bf16[256,512]{1,0:T(8,128)(2,1)S(1)}, u32[]{:S(2)}, u32[]{:S(2)}) collective-permute-start(bf16[256,512]{1,0:T(8,128)(2,1)S(1)} %collective-permute-done.refs_1_), channel_id=1, source_target_pairs={{0,8},{8,16},{16,24},{24,0},{1,9},{9,17},{17,25},{25,1},{2,10},{10... | collective-permute-start | bytes 786440 | tf_op jit(solution)/shard_map/ppermute | solution.py:14
  28.6 14.4 %collective-permute-start.6 = (bf16[256,512]{1,0:T(8,128)(2,1)S(1)}, bf16[256,512]{1,0:T(8,128)(2,1)S(1)}, u32[]{:S(2)}, u32[]{:S(2)}) collective-permute-start(bf16[256,512]{1,0:T(8,128)(2,1)S(1)} %collective-permute-done.5.refs_1_), channel_id=1, source_target_pairs={{0,8},{8,16},{16,24},{24,0},{1,9},{9,17},{17,25},{25,1},{2,10},{10... | collective-permute-start | bytes 786440 | tf_op jit(solution)/shard_map/ppermute | solution.py:14
  37.4 8.6 %collective-permute-start.2 = (bf16[256,512]{1,0:T(8,128)(2,1)S(1)}, bf16[256,512]{1,0:T(8,128)(2,1)S(1)}, u32[]{:S(2)}, u32[]{:S(2)}) collective-permute-start(bf16[256,512]{1,0:T(8,128)(2,1)S(1)} %collective-permute-done.1.refs_2_), channel_id=1, source_target_pairs={{0,8},{8,16},{16,24},{24,0},{1,9},{9,17},{17,25},{25,1},{2,10},{10... | collective-permute-start | bytes 786440 | tf_op jit(solution)/shard_map/ppermute | solution.py:14
  37.9 8.1 %collective-permute-start.18 = (bf16[2,128,512]{2,1,0:T(8,128)(2,1)S(1)}, bf16[2,128,512]{2,1,0:T(8,128)(2,1)S(1)}, u32[]{:S(2)}, u32[]{:S(2)}) collective-permute-start(bf16[2,128,512]{2,1,0:T(8,128)(2,1)S(1)} %get-tuple-element.51), channel_id=1, source_target_pairs={{0,4},{4,0},{1,5},{5,1},{2,6},{6,2},{3,7},{7,3},{8,12},{12,8},{9,1... | collective-permute-start | bytes 786440 | tf_op jit(solution)/shard_map/ppermute | solution.py:14
  39.5 9.2 %collective-permute-start.19 = (bf16[2,128,512]{2,1,0:T(8,128)(2,1)S(1)}, bf16[2,128,512]{2,1,0:T(8,128)(2,1)S(1)}, u32[]{:S(2)}, u32[]{:S(2)}) collective-permute-start(bf16[2,128,512]{2,1,0:T(8,128)(2,1)S(1)} %get-tuple-element.52), channel_id=1, source_target_pairs={{0,2},{2,0},{1,3},{3,1},{4,6},{6,4},{5,7},{7,5},{8,10},{10,8},{9,1... | collective-permute-start | bytes 786440 | tf_op jit(solution)/shard_map/ppermute | solution.py:14
  41.5 8.7 %collective-permute-start.16 = (bf16[2,128,512]{2,1,0:T(8,128)(2,1)S(1)}, bf16[2,128,512]{2,1,0:T(8,128)(2,1)S(1)}, u32[]{:S(2)}, u32[]{:S(2)}) collective-permute-start(bf16[2,128,512]{2,1,0:T(8,128)(2,1)S(1)} %get-tuple-element.56), channel_id=1, source_target_pairs={{0,4},{4,0},{1,5},{5,1},{2,6},{6,2},{3,7},{7,3},{8,12},{12,8},{9,1... | collective-permute-start | bytes 786440 | tf_op jit(solution)/shard_map/ppermute | solution.py:14
  43.0 9.6 %collective-permute-start.17 = (bf16[2,128,512]{2,1,0:T(8,128)(2,1)S(1)}, bf16[2,128,512]{2,1,0:T(8,128)(2,1)S(1)}, u32[]{:S(2)}, u32[]{:S(2)}) collective-permute-start(bf16[2,128,512]{2,1,0:T(8,128)(2,1)S(1)} %get-tuple-element.57), channel_id=1, source_target_pairs={{0,2},{2,0},{1,3},{3,1},{4,6},{6,4},{5,7},{7,5},{8,10},{10,8},{9,1... | collective-permute-start | bytes 786440 | tf_op jit(solution)/shard_map/ppermute | solution.py:14
  46.0 14.3 %collective-permute-start.7 = (bf16[256,512]{1,0:T(8,128)(2,1)S(1)}, bf16[256,512]{1,0:T(8,128)(2,1)S(1)}, u32[]{:S(2)}, u32[]{:S(2)}) collective-permute-start(bf16[256,512]{1,0:T(8,128)(2,1)S(1)} %collective-permute-done.6.refs_2_), channel_id=1, source_target_pairs={{0,8},{8,16},{16,24},{24,0},{1,9},{9,17},{17,25},{25,1},{2,10},{10... | collective-permute-start | bytes 786440 | tf_op jit(solution)/shard_map/ppermute | solution.py:14
  50.2 31.7 %copy-start.2 = (f32[256,512]{1,0:T(8,128)S(1)}, f32[256,512]{1,0:T(8,128)}, u32[]{:S(2)}) copy-start(f32[256,512]{1,0:T(8,128)} %master.1) | copy-start | bytes 1572868
  50.2 31.7 %copy-start.3 = (f32[256,512]{1,0:T(8,128)S(1)}, f32[256,512]{1,0:T(8,128)}, u32[]{:S(2)}) copy-start(f32[256,512]{1,0:T(8,128)} %moment_one.1) | copy-start | bytes 1572868
  50.2 31.7 %copy-start.4 = (f32[256,512]{1,0:T(8,128)S(1)}, f32[256,512]{1,0:T(8,128)}, u32[]{:S(2)}) copy-start(f32[256,512]{1,0:T(8,128)} %moment_two.1) | copy-start | bytes 1572868
  53.0 30.5 %collective-permute-start.22 = (bf16[4,256,512]{2,1,0:T(8,128)(2,1)S(1)}, bf16[4,256,512]{2,1,0:T(8,128)(2,1)S(1)}, u32[]{:S(2)}, u32[]{:S(2)}) collective-permute-start(bf16[4,256,512]{2,1,0:T(8,128)(2,1)S(1)} %shard_map.137.refs_3_), channel_id=1, source_target_pairs={{0,4},{4,0},{1,5},{5,1},{2,6},{6,2},{3,7},{7,3},{8,12},{12,8},{9,1... | collective-permute-start | bytes 3145736 | tf_op jit(solution)/shard_map/ppermute | solution.py:14
  55.0 28.9 %collective-permute-start.20 = (bf16[4,256,512]{2,1,0:T(8,128)(2,1)S(1)}, bf16[4,256,512]{2,1,0:T(8,128)(2,1)S(1)}, u32[]{:S(2)}, u32[]{:S(2)}) collective-permute-start(bf16[4,256,512]{2,1,0:T(8,128)(2,1)S(1)} %shard_map.137.refs_3_), channel_id=1, source_target_pairs={{0,2},{2,0},{1,3},{3,1},{4,6},{6,4},{5,7},{7,5},{8,10},{10,8},{9,1... | collective-permute-start | bytes 3145736 | tf_op jit(solution)/shard_map/ppermute | solution.py:14
  56.5 11.0 %collective-permute-start.24 = (bf16[256,512]{1,0:T(8,128)(2,1)S(1)}, bf16[256,512]{1,0:T(8,128)(2,1)S(1)}, u32[]{:S(2)}, u32[]{:S(2)}) collective-permute-start(bf16[256,512]{1,0:T(8,128)(2,1)S(1)} %get-tuple-element.59), channel_id=1, source_target_pairs={{0,8},{8,16},{16,24},{24,0},{1,9},{9,17},{17,25},{25,1},{2,10},{10... | collective-permute-start | bytes 786440 | tf_op jit(solution)/shard_map/ppermute | solution.py:14
  58.1 12.4 %collective-permute-start.25 = (bf16[256,512]{1,0:T(8,128)(2,1)S(1)}, bf16[256,512]{1,0:T(8,128)(2,1)S(1)}, u32[]{:S(2)}, u32[]{:S(2)}) collective-permute-start(bf16[256,512]{1,0:T(8,128)(2,1)S(1)} %get-tuple-element.60), channel_id=1, source_target_pairs={{0,24},{8,0},{16,8},{24,16},{1,25},{9,1},{17,9},{25,17},{2,26},{10... | collective-permute-start | bytes 786440 | tf_op jit(solution)/shard_map/ppermute | solution.py:14
  60.3 21.6 %collective-permute-start.26 = (bf16[256,512]{1,0:T(8,128)(2,1)S(1)}, bf16[256,512]{1,0:T(8,128)(2,1)S(1)}, u32[]{:S(2)}, u32[]{:S(2)}) collective-permute-start(bf16[256,512]{1,0:T(8,128)(2,1)S(1)} %shard_map.145), channel_id=1, source_target_pairs={{0,16},{8,24},{16,0},{24,8},{1,17},{9,25},{17,1},{25,9},{2,18},{10... | collective-permute-start | bytes 786440 | tf_op jit(solution)/shard_map/ppermute | solution.py:14
  61.2 30.0 %copy-start.1 = (bf16[256,8192]{1,0:T(8,128)(2,1)S(1)}, bf16[256,8192]{1,0:T(8,128)(2,1)}, u32[]{:S(2)}) copy-start(bf16[256,8192]{1,0:T(8,128)(2,1)} %refs_0_.6) | copy-start | bytes 12582916
  82.8 2.4 %collective-permute-start.27 = (bf16[3,256,512]{2,1,0:T(8,128)(2,1)S(1)}, bf16[3,256,512]{2,1,0:T(8,128)(2,1)S(1)}, u32[]{:S(2)}, u32[]{:S(2)}) collective-permute-start(bf16[3,256,512]{2,1,0:T(8,128)(2,1)S(1)} %get-tuple-element.67.refs_1_), channel_id=1, source_target_pairs={{0,1},{1,0},{2,3},{3,2},{4,5},{5,4},{6,7},{7,6},{8,9},{9,8},{10,11... | collective-permute-start | bytes 2359304 | tf_op jit(solution)/shard_map/ppermute | solution.py:14
  82.9 4.2 %collective-permute-start.3 = (bf16[4,256,512]{2,1,0:T(8,128)(2,1)S(1)}, bf16[4,256,512]{2,1,0:T(8,128)(2,1)S(1)}, u32[]{:S(2)}, u32[]{:S(2)}) collective-permute-start(bf16[4,256,512]{2,1,0:T(8,128)(2,1)S(1)} %shard_map.137.refs_3_), channel_id=1, source_target_pairs={{0,1},{1,0},{2,3},{3,2},{4,5},{5,4},{6,7},{7,6},{8,9},{9,8},{10,11... | collective-permute-start | bytes 3145736 | tf_op jit(solution)/shard_map/ppermute | solution.py:14
  83.4 4.8 %collective-permute-start.8 = (bf16[4,256,512]{2,1,0:T(8,128)(2,1)S(1)}, bf16[4,256,512]{2,1,0:T(8,128)(2,1)S(1)}, u32[]{:S(2)}, u32[]{:S(2)}) collective-permute-start(bf16[4,256,512]{2,1,0:T(8,128)(2,1)S(1)} %shard_map.138.refs_5_), channel_id=1, source_target_pairs={{0,1},{1,0},{2,3},{3,2},{4,5},{5,4},{6,7},{7,6},{8,9},{9,8},{10,11... | collective-permute-start | bytes 3145736 | tf_op jit(solution)/shard_map/ppermute | solution.py:14
  83.5 6.2 %collective-permute-start.23 = (bf16[4,256,512]{2,1,0:T(8,128)(2,1)S(1)}, bf16[4,256,512]{2,1,0:T(8,128)(2,1)S(1)}, u32[]{:S(2)}, u32[]{:S(2)}) collective-permute-start(bf16[4,256,512]{2,1,0:T(8,128)(2,1)S(1)} %collective-permute-done.22.refs_9_), channel_id=1, source_target_pairs={{0,1},{1,0},{2,3},{3,2},{4,5},{5,4},{6,7},{7,6},{8,9},{9,8},{10,11... | collective-permute-start | bytes 3145736 | tf_op jit(solution)/shard_map/ppermute | solution.py:14
  83.9 7.3 %collective-permute-start.21 = (bf16[4,256,512]{2,1,0:T(8,128)(2,1)S(1)}, bf16[4,256,512]{2,1,0:T(8,128)(2,1)S(1)}, u32[]{:S(2)}, u32[]{:S(2)}) collective-permute-start(bf16[4,256,512]{2,1,0:T(8,128)(2,1)S(1)} %collective-permute-done.20.refs_7_), channel_id=1, source_target_pairs={{0,1},{1,0},{2,3},{3,2},{4,5},{5,4},{6,7},{7,6},{8,9},{9,8},{10,11... | collective-permute-start | bytes 3145736 | tf_op jit(solution)/shard_map/ppermute | solution.py:14
  85.2 19.6 %collective-permute-start.28 = (bf16[3,256,512]{2,1,0:T(8,128)(2,1)S(1)}, bf16[3,256,512]{2,1,0:T(8,128)(2,1)S(1)}, u32[]{:S(2)}, u32[]{:S(2)}) collective-permute-start(bf16[3,256,512]{2,1,0:T(8,128)(2,1)S(1)} %get-tuple-element.67.refs_1_), channel_id=1, source_target_pairs={{0,2},{2,0},{1,3},{3,1},{4,6},{6,4},{5,7},{7,5},{8,10},{10,8},{9,1... | collective-permute-start | bytes 2359304 | tf_op jit(solution)/shard_map/ppermute | solution.py:14
  91.2 15.9 %copy-start.7 = (s32[4]{0:T(128)S(1)}, s32[4]{0:T(128)}, u32[]{:S(2)}) copy-start(s32[4]{0:T(128)} %refs_0_.7) | copy-start | bytes 52
  104.8 2.3 %collective-permute-start.29 = (bf16[3,256,512]{2,1,0:T(8,128)(2,1)S(1)}, bf16[3,256,512]{2,1,0:T(8,128)(2,1)S(1)}, u32[]{:S(2)}, u32[]{:S(2)}) collective-permute-start(bf16[3,256,512]{2,1,0:T(8,128)(2,1)S(1)} %collective-permute-done.28.refs_3_), channel_id=1, source_target_pairs={{0,1},{1,0},{2,3},{3,2},{4,5},{5,4},{6,7},{7,6},{8,9},{9,8},{10,11... | collective-permute-start | bytes 2359304 | tf_op jit(solution)/shard_map/ppermute | solution.py:14

commit v2 on v1

--- a/solution.py
+++ b/solution.py
@@ -374,7 +374,28 @@
     def simple(body, outs, *operands, limit=12, **more):
         return local(body, outs, 8, 8, limit, *operands, **more)
 
-    quarter, = simple(lambda *refs: quarter_body(rows, *refs), [((rows, width), low)], weight)
+    ours, soon, later, rstd = prepare(tokens, rows, order)
+    flags, = simple(
+        lambda *refs: flags_body(many, *refs),
+        [((24, width), full)],
+        after(live, soon),
+        scalars=1,
+    )
+    grads = key_grad, shift(after(key_grad, soon), "c", 1)
+    theirs = shift(soon, "c", 1), shift(after(later, grads[1]), "c", 1)
+    cores = (flags, ours, *theirs, *grads)
+
+    groups = order[: planes // 2], order[planes // 2 :]
+    came, made = [], []
+    for group, part in zip(groups, theirs):
+        to_x, to_y = simple(
+            lambda *refs: first_body(order, rows, group, *refs),
+            [((2, len(group), half, width), low)] * 2,
+            flags, ours, part, *grads,
+        )
+        made.append(to_x)
+        came.append((shift(to_x, "x", 1), shift(to_y, "y", 1)))
+    quarter, = simple(lambda *refs: quarter_body(rows, *refs), [((rows, width), low)], after(weight, made[0]))
     opposite = lax.ppermute(quarter, ("y", "x"), [(0, 3), (1, 2), (2, 1), (3, 0)])
     quarters, opposites = [quarter], [opposite]
     for by in range(1, planes):
@@ -387,30 +408,10 @@
     )
     corner, = simple(stack_body, [((planes, rows, width), low)], *opposites)
 
-    ours, soon, later, rstd = prepare(tokens, rows, order)
-    flags, = simple(
-        lambda *refs: flags_body(many, *refs),
-        [((24, width), full)],
-        after(live, soon),
-        scalars=1,
-    )
-    grads = key_grad, shift(after(key_grad, soon), "c", 1)
-    theirs = shift(soon, "c", 1), shift(after(later, grads[1]), "c", 1)
-    cores = (flags, ours, *theirs, *grads)
-
-    groups = order[: planes // 2], order[planes // 2 :]
-    came = []
-    for group, part in zip(groups, theirs):
-        to_x, to_y = simple(
-            lambda *refs: first_body(order, rows, group, *refs),
-            [((2, len(group), half, width), low)] * 2,
-            flags, ours, part, *grads,
-        )
-        came.append((shift(to_x, "x", 1), shift(to_y, "y", 1)))
     late = []
     along_z = []
     first_out = ()
-    for group, (from_x, from_y), ties in zip(groups, came, ((), quarters[1:3])):
+    for group, (from_x, from_y), ties in zip(groups, came, (quarters[1:3], ())):
         to_y, to_x = simple(
             lambda *refs: second_body(order, rows, group, *refs),
             [((len(group), half, width), low)] * 2,
@@ -435,9 +436,12 @@
         *cores, *came[1], *late[1], master, moment_one, moment_two, *along_z,
     )
 
+    beside = shift(state, "c", 1)
+    across = shift(state, "x", 1)
     pieces, where = [], []
     for fy, fx, piece in ((0, 0, column), (1, 1, corner), (0, 1, over_x), (1, 0, over_y)):
-        pieces += [piece, shift(piece, "c", 1)]
+        fetched = piece is over_x or piece is over_y
+        pieces += [piece, shift(after(piece, beside) if fetched else piece, "c", 1)]
         where += [[(by, fy, fx, fc) for by in range(planes)] for fc in (0, 1)]
     keys, input_grad = pl.pallas_call(
         lambda *refs: both_ways_body(planes, rows, where, *refs),
@@ -455,8 +459,6 @@
         compiler_params=pltpu.CompilerParams(vmem_limit_bytes=24 * MIB),
     )(tokens, key_grad, rstd, *pieces)
 
-    beside = shift(state, "c", 1)
-    across = shift(after(state, beside), "x", 1)
     new_master, new_one, new_two = simple(
         update_body, [((rows, width), full)] * 3, grad, master, moment_one, moment_two
     )

time: 109 us -> 111 us (1.018)
  waiting for transfers between devices: 60.6 us -> 65.3 us
  starting transfers between devices: 29.4 us -> 26.3 us
    ppermute x1, waiting for transfers between devices: 3.04 us -> 9.64 us  [on_device(): lax.ppermute(quarter, ('y', 'x'), [(0, 3), (1, 2), (2, 1), (3, 0)])]
    ppermute x1, starting transfers between devices: 3.66 us -> 1.5 us  [on_device(): lax.ppermute(quarter, ('y', 'x'), [(0, 3), (1, 2), (2, 1), (3, 0)])]
    ppermute x29, waiting for transfers between devices: 57.6 us -> 55.7 us  [shift(): lax.ppermute(value, axis, [(i, (i + by) % size) for i in range(size)])]
  transfers between devices with their start and end apart: 30 -> 30, of which waited for: 19 -> 17; matrix products, arithmetic and copies ran while one was open for 0% -> 0% of each run, Pallas kernels for 12% -> 12%
where the time goes in v2:
time: 111 us
  waiting for transfers between devices  65.3 us (59%)
  starting transfers between devices  26.3 us (24%)
  Pallas kernels  18.4 us (17%)
    ppermute x29, waiting for transfers between devices, shift(): lax.ppermute(value, axis, [(i, (i + by) % size) for i in range(size)])  55.7 us
    ppermute x29, starting transfers between devices, shift(): lax.ppermute(value, axis, [(i, (i + by) % size) for i in range(size)])  24.8 us
    ppermute x1, waiting for transfers between devices, on_device(): lax.ppermute(quarter, ('y', 'x'), [(0, 3), (1, 2), (2, 1), (3, 0)])  9.64 us
    pallas_call x13, Pallas kernels, local(): pl.pallas_call(body, out_shape=[jax.ShapeDtypeStruct(s, t) for s, t in ou...  8.75 us
    pallas_call x1, Pallas kernels, on_device(): pl.pallas_call(lambda *refs: both_ways_body(planes, rows, where, *refs),...  6.42 us
    pallas_call x1, Pallas kernels, prepare(): pl.pallas_call(lambda *refs: prepare_body(rows, order, *refs), out_shape=...  3.27 us
  transfers between devices with their start and end apart: 30, of which 17 were waited for; matrix products, arithmetic and copies ran while one was open for 0% of the time, Pallas kernels for 12%

profile of v2, /device:TPU:0, one launch (start us, length us, event | category | flops | bytes accessed | tf_op | source)
XLA Modules:
  0.0 110.9 jit_solution(12659864044308063253)
XLA Ops:
  0.7 3.3 %shard_map.135 = (bf16[256,4096]{1,0:T(8,128)(2,1)S(1)}, bf16[256,2048]{1,0:T(8,128)(2,1)S(1)}, bf16[256,2048]{1,0:T(8,128)(2,1)S(1)}, f32[256,1]{1,0:T(8,128)S(1)}) custom-call(bf16[256,8192]{1,0:T(8,128)(2,1)} %refs_0_.5), custom_call_target="tpu_custom_call" | custom-call | flops 8 | bytes 8 | tf_op jit(solution)/shard_map/pallas_call | solution.py:183
  3.9 0.5 collective-permute-start
  4.5 0.1 collective-permute-start.1
  4.5 2.6 %collective-permute-done.1.refs_4_.refs_5_ = bf16[256,512]{1,0:T(8,128)(2,1)S(1)} collective-permute-done((bf16[256,512]{1,0:T(8,128)(2,1)S(1)}, bf16[256,512]{1,0:T(8,128)(2,1)S(1)}, u32[]{:S(2)}, u32[]{:S(2)}) %collective-permute-start.1) | collective-permute-done | bytes 262176 | tf_op jit(solution)/shard_map/ppermute | solution.py:14
  7.1 0.4 collective-permute-start.11
  7.5 0.6 shard_map.136.refs_0_
  8.1 0.0 collective-permute-done.refs_2_
  8.1 0.8 shard_map.137
  8.9 2.7 %collective-permute-start.13 = (bf16[2,2,128,512]{3,2,1,0:T(8,128)(2,1)S(1)}, bf16[2,2,128,512]{3,2,1,0:T(8,128)(2,1)S(1)}, u32[]{:S(2)}, u32[]{:S(2)}) collective-permute-start(bf16[2,2,128,512]{3,2,1,0:T(8,128)(2,1)S(1)} %get-tuple-element.48), channel_id=1, source_target_pairs={{0,2},{2,0},{1,3},{3,1},{4,6},{6,4},{5,7},{7,5},{8,10},{10,8},{9,1... | collective-permute-start | bytes 1572872 | tf_op jit(solution)/shard_map/ppermute | solution.py:14
  11.6 1.6 %collective-permute-start.2 = (bf16[256,512]{1,0:T(8,128)(2,1)S(1)}, bf16[256,512]{1,0:T(8,128)(2,1)S(1)}, u32[]{:S(2)}, u32[]{:S(2)}) collective-permute-start(bf16[256,512]{1,0:T(8,128)(2,1)S(1)} %shard_map.138.refs_0_), channel_id=1, source_target_pairs={{0,8},{8,16},{16,24},{24,0},{1,9},{9,17},{17,25},{25,1},{2,10},{10... | collective-permute-start | bytes 786440 | tf_op jit(solution)/shard_map/ppermute | solution.py:14
  13.3 1.5 %collective-permute-start.6 = (bf16[256,512]{1,0:T(8,128)(2,1)S(1)}, bf16[256,512]{1,0:T(8,128)(2,1)S(1)}, u32[]{:S(2)}, u32[]{:S(2)}) collective-permute-start(bf16[256,512]{1,0:T(8,128)(2,1)S(1)} %shard_map.138.refs_0_), channel_id=1, source_target_pairs={{0,6},{2,4},{4,2},{6,0},{1,7},{3,5},{5,3},{7,1},{8,14},{10,12},{12... | collective-permute-start | bytes 786440 | tf_op jit(solution)/shard_map/ppermute | solution.py:399
  14.8 0.5 collective-permute-start.14
  15.3 0.0 collective-permute-done.11.refs_2_.refs_3_
  15.3 0.8 shard_map.141
  16.0 1.6 %collective-permute-start.12 = (bf16[2,2,128,512]{3,2,1,0:T(8,128)(2,1)S(1)}, bf16[2,2,128,512]{3,2,1,0:T(8,128)(2,1)S(1)}, u32[]{:S(2)}, u32[]{:S(2)}) collective-permute-start(bf16[2,2,128,512]{3,2,1,0:T(8,128)(2,1)S(1)} %get-tuple-element.52), channel_id=1, source_target_pairs={{0,2},{2,0},{1,3},{3,1},{4,6},{6,4},{5,7},{7,5},{8,10},{10,8},{9,1... | collective-permute-start | bytes 1572872 | tf_op jit(solution)/shard_map/ppermute | solution.py:14
  17.6 4.2 %collective-permute-done.2.refs_1_ = bf16[256,512]{1,0:T(8,128)(2,1)S(1)} collective-permute-done((bf16[256,512]{1,0:T(8,128)(2,1)S(1)}, bf16[256,512]{1,0:T(8,128)(2,1)S(1)}, u32[]{:S(2)}, u32[]{:S(2)}) %collective-permute-start.2) | collective-permute-done | bytes 262176 | tf_op jit(solution)/shard_map/ppermute | solution.py:14
  21.8 0.0 collective-permute-start.3
  21.8 9.6 %collective-permute-done.6.refs_0_ = bf16[256,512]{1,0:T(8,128)(2,1)S(1)} collective-permute-done((bf16[256,512]{1,0:T(8,128)(2,1)S(1)}, bf16[256,512]{1,0:T(8,128)(2,1)S(1)}, u32[]{:S(2)}, u32[]{:S(2)}) %collective-permute-start.6) | collective-permute-done | bytes 262176 | tf_op jit(solution)/shard_map/ppermute | solution.py:399
  31.5 0.0 collective-permute-start.15
  31.5 2.1 %collective-permute-start.7 = (bf16[256,512]{1,0:T(8,128)(2,1)S(1)}, bf16[256,512]{1,0:T(8,128)(2,1)S(1)}, u32[]{:S(2)}, u32[]{:S(2)}) collective-permute-start(bf16[256,512]{1,0:T(8,128)(2,1)S(1)} %collective-permute-done.6.refs_0_), channel_id=1, source_target_pairs={{0,8},{8,16},{16,24},{24,0},{1,9},{9,17},{17,25},{25,1},{2,10},{10... | collective-permute-start | bytes 786440 | tf_op jit(solution)/shard_map/ppermute | solution.py:14
  33.6 0.7 collective-permute-done.14.refs_7_
  34.3 0.0 collective-permute-done.3.refs_2_
  34.3 0.5 shard_map.142
  34.8 0.9 collective-permute-start.18
  35.7 5.1 %collective-permute-done.7.refs_1_ = bf16[256,512]{1,0:T(8,128)(2,1)S(1)} collective-permute-done((bf16[256,512]{1,0:T(8,128)(2,1)S(1)}, bf16[256,512]{1,0:T(8,128)(2,1)S(1)}, u32[]{:S(2)}, u32[]{:S(2)}) %collective-permute-start.7) | collective-permute-done | bytes 262176 | tf_op jit(solution)/shard_map/ppermute | solution.py:14
  40.8 1.3 %collective-permute-start.4 = (bf16[256,512]{1,0:T(8,128)(2,1)S(1)}, bf16[256,512]{1,0:T(8,128)(2,1)S(1)}, u32[]{:S(2)}, u32[]{:S(2)}) collective-permute-start(bf16[256,512]{1,0:T(8,128)(2,1)S(1)} %collective-permute-done.3.refs_2_), channel_id=1, source_target_pairs={{0,8},{8,16},{16,24},{24,0},{1,9},{9,17},{17,25},{25,1},{2,10},{10... | collective-permute-start | bytes 786440 | tf_op jit(solution)/shard_map/ppermute | solution.py:14
  42.1 1.5 %collective-permute-start.19 = (bf16[2,128,512]{2,1,0:T(8,128)(2,1)S(1)}, bf16[2,128,512]{2,1,0:T(8,128)(2,1)S(1)}, u32[]{:S(2)}, u32[]{:S(2)}) collective-permute-start(bf16[2,128,512]{2,1,0:T(8,128)(2,1)S(1)} %get-tuple-element.56), channel_id=1, source_target_pairs={{0,2},{2,0},{1,3},{3,1},{4,6},{6,4},{5,7},{7,5},{8,10},{10,8},{9,1... | collective-permute-start | bytes 786440 | tf_op jit(solution)/shard_map/ppermute | solution.py:14
  43.6 2.8 %collective-permute-done.15.refs_7_ = bf16[2,2,128,512]{3,2,1,0:T(8,128)(2,1)S(1)} collective-permute-done((bf16[2,2,128,512]{3,2,1,0:T(8,128)(2,1)S(1)}, bf16[2,2,128,512]{3,2,1,0:T(8,128)(2,1)S(1)}, u32[]{:S(2)}, u32[]{:S(2)}) %collective-permute-start.15) | collective-permute-done | bytes 524320 | tf_op jit(solution)/shard_map/ppermute | solution.py:14
  46.3 0.5 shard_map.143
  46.8 0.1 collective-permute-start.16
  46.9 5.0 %collective-permute-done.18.refs_8_ = bf16[2,128,512]{2,1,0:T(8,128)(2,1)S(1)} collective-permute-done((bf16[2,128,512]{2,1,0:T(8,128)(2,1)S(1)}, bf16[2,128,512]{2,1,0:T(8,128)(2,1)S(1)}, u32[]{:S(2)}, u32[]{:S(2)}) %collective-permute-start.18) | collective-permute-done | bytes 262176 | tf_op jit(solution)/shard_map/ppermute | solution.py:14
  52.0 1.5 %collective-permute-start.17 = (bf16[2,128,512]{2,1,0:T(8,128)(2,1)S(1)}, bf16[2,128,512]{2,1,0:T(8,128)(2,1)S(1)}, u32[]{:S(2)}, u32[]{:S(2)}) collective-permute-start(bf16[2,128,512]{2,1,0:T(8,128)(2,1)S(1)} %get-tuple-element.60), channel_id=1, source_target_pairs={{0,2},{2,0},{1,3},{3,1},{4,6},{6,4},{5,7},{7,5},{8,10},{10,8},{9,1... | collective-permute-start | bytes 786440 | tf_op jit(solution)/shard_map/ppermute | solution.py:14
  53.4 1.6 %collective-permute-start.9 = (bf16[256,512]{1,0:T(8,128)(2,1)S(1)}, bf16[256,512]{1,0:T(8,128)(2,1)S(1)}, u32[]{:S(2)}, u32[]{:S(2)}) collective-permute-start(bf16[256,512]{1,0:T(8,128)(2,1)S(1)} %collective-permute-done.8.refs_2_), channel_id=1, source_target_pairs={{0,8},{8,16},{16,24},{24,0},{1,9},{9,17},{17,25},{25,1},{2,10},{10... | collective-permute-start | bytes 786440 | tf_op jit(solution)/shard_map/ppermute | solution.py:14
  55.0 0.0 collective-permute-done.19.refs_9_
  55.0 0.6 shard_map.144
  55.6 1.6 %collective-permute-start.21 = (bf16[256,512]{1,0:T(8,128)(2,1)S(1)}, bf16[256,512]{1,0:T(8,128)(2,1)S(1)}, u32[]{:S(2)}, u32[]{:S(2)}) collective-permute-start(bf16[256,512]{1,0:T(8,128)(2,1)S(1)} %get-tuple-element.62), channel_id=1, source_target_pairs={{0,8},{8,16},{16,24},{24,0},{1,9},{9,17},{17,25},{25,1},{2,10},{10... | collective-permute-start | bytes 786440 | tf_op jit(solution)/shard_map/ppermute | solution.py:14
  57.2 2.2 %collective-permute-start.22 = (bf16[256,512]{1,0:T(8,128)(2,1)S(1)}, bf16[256,512]{1,0:T(8,128)(2,1)S(1)}, u32[]{:S(2)}, u32[]{:S(2)}) collective-permute-start(bf16[256,512]{1,0:T(8,128)(2,1)S(1)} %get-tuple-element.63), channel_id=1, source_target_pairs={{0,24},{8,0},{16,8},{24,16},{1,25},{9,1},{17,9},{25,17},{2,26},{10... | collective-permute-start | bytes 786440 | tf_op jit(solution)/shard_map/ppermute | solution.py:14
  59.5 0.4 shard_map.145
  59.9 1.5 %collective-permute-start.23 = (bf16[256,512]{1,0:T(8,128)(2,1)S(1)}, bf16[256,512]{1,0:T(8,128)(2,1)S(1)}, u32[]{:S(2)}, u32[]{:S(2)}) collective-permute-start(bf16[256,512]{1,0:T(8,128)(2,1)S(1)} %shard_map.145), channel_id=1, source_target_pairs={{0,16},{8,24},{16,0},{24,8},{1,17},{9,25},{17,1},{25,9},{2,18},{10... | collective-permute-start | bytes 786440 | tf_op jit(solution)/shard_map/ppermute | solution.py:14
  61.4 0.1 shard_map.139.refs_3_
  61.4 0.6 collective-permute-start.26
  62.0 2.5 %collective-permute-done.9.refs_3_ = bf16[256,512]{1,0:T(8,128)(2,1)S(1)} collective-permute-done((bf16[256,512]{1,0:T(8,128)(2,1)S(1)}, bf16[256,512]{1,0:T(8,128)(2,1)S(1)}, u32[]{:S(2)}, u32[]{:S(2)}) %collective-permute-start.9) | collective-permute-done | bytes 262176 | tf_op jit(solution)/shard_map/ppermute | solution.py:14
  64.5 0.5 collective-permute-start.20
  65.0 0.1 shard_map.140.refs_5_
  65.1 0.0 copy-start.1
  65.1 5.0 %collective-permute-done.21.refs_13_ = bf16[256,512]{1,0:T(8,128)(2,1)S(1)} collective-permute-done((bf16[256,512]{1,0:T(8,128)(2,1)S(1)}, bf16[256,512]{1,0:T(8,128)(2,1)S(1)}, u32[]{:S(2)}, u32[]{:S(2)}) %collective-permute-start.21) | collective-permute-done | bytes 262176 | tf_op jit(solution)/shard_map/ppermute | solution.py:14
  70.2 1.8 %collective-permute-done.22.refs_14_ = bf16[256,512]{1,0:T(8,128)(2,1)S(1)} collective-permute-done((bf16[256,512]{1,0:T(8,128)(2,1)S(1)}, bf16[256,512]{1,0:T(8,128)(2,1)S(1)}, u32[]{:S(2)}, u32[]{:S(2)}) %collective-permute-start.22) | collective-permute-done | bytes 262176 | tf_op jit(solution)/shard_map/ppermute | solution.py:14
  71.9 11.1 %collective-permute-done.23.refs_15_ = bf16[256,512]{1,0:T(8,128)(2,1)S(1)} collective-permute-done((bf16[256,512]{1,0:T(8,128)(2,1)S(1)}, bf16[256,512]{1,0:T(8,128)(2,1)S(1)}, u32[]{:S(2)}, u32[]{:S(2)}) %collective-permute-start.23) | collective-permute-done | bytes 262176 | tf_op jit(solution)/shard_map/ppermute | solution.py:14
  83.0 0.9 shard_map.146
  83.9 0.1 collective-permute-start.24
  84.0 0.5 collective-permute-start.5
  84.5 0.1 collective-permute-start.10
  84.6 1.7 %collective-permute-done.24.refs_2_ = bf16[3,256,512]{2,1,0:T(8,128)(2,1)S(1)} collective-permute-done((bf16[3,256,512]{2,1,0:T(8,128)(2,1)S(1)}, bf16[3,256,512]{2,1,0:T(8,128)(2,1)S(1)}, u32[]{:S(2)}, u32[]{:S(2)}) %collective-permute-start.24) | collective-permute-done | bytes 786464 | tf_op jit(solution)/shard_map/ppermute | solution.py:14
  86.3 0.1 collective-permute-start.27
  86.4 0.4 collective-permute-start.25
  86.8 0.9 collective-permute-start.28
  87.7 1.4 %shard_map.148 = (f32[256,512]{1,0:T(8,128)}, f32[256,512]{1,0:T(8,128)}, f32[256,512]{1,0:T(8,128)}) custom-call(f32[256,512]{1,0:T(8,128)S(1)} %get-tuple-element.72.grad, f32[256,512]{1,0:T(8,128)S(1)} %copy-done.2, f32[256,512]{1,0:T(8,128)S(1)} %copy-done.3, f32[256,512]{1,0:T(8,128)S(1)} %copy-done.4), custom_call_target="tpu_custom_call" | custom-call | flops 8 | bytes 8 | tf_op jit(solution)/shard_map/pallas_call | solution.py:115
  89.0 0.3 collective-permute-done.10.refs_6_
  89.3 1.5 %collective-permute-done.27.refs_10_ = bf16[4,256,512]{2,1,0:T(8,128)(2,1)S(1)} collective-permute-done((bf16[4,256,512]{2,1,0:T(8,128)(2,1)S(1)}, bf16[4,256,512]{2,1,0:T(8,128)(2,1)S(1)}, u32[]{:S(2)}, u32[]{:S(2)}) %collective-permute-start.27) | collective-permute-done | bytes 1048608 | tf_op jit(solution)/shard_map/ppermute | solution.py:14
  90.8 1.5 %collective-permute-done.25.refs_8_ = bf16[4,256,512]{2,1,0:T(8,128)(2,1)S(1)} collective-permute-done((bf16[4,256,512]{2,1,0:T(8,128)(2,1)S(1)}, bf16[4,256,512]{2,1,0:T(8,128)(2,1)S(1)}, u32[]{:S(2)}, u32[]{:S(2)}) %collective-permute-start.25) | collective-permute-done | bytes 1048608 | tf_op jit(solution)/shard_map/ppermute | solution.py:14
  92.3 6.4 %shard_map.147 = (bf16[256,512]{1,0:T(8,128)(2,1)}, bf16[256,8192]{1,0:T(8,128)(2,1)}) custom-call(bf16[256,8192]{1,0:T(8,128)(2,1)S(1)} %copy-done.1, bf16[256,512]{1,0:T(8,128)(2,1)S(1)} %copy-done, f32[256,1]{1,0:T(8,128)S(1)} %get-tuple-element.43.refs_2_, bf16[4,256,512]{2,1,0:T(8,128)(2,1)S(1)} %shard_map.139.refs_3_, ...), custom_call_target="tpu_custom_call" | custom-call | flops 8 | bytes 8 | tf_op jit(solution)/shard_map/pallas_call | solution.py:446
  98.7 7.7 %collective-permute-done.28.refs_3_ = bf16[3,256,512]{2,1,0:T(8,128)(2,1)S(1)} collective-permute-done((bf16[3,256,512]{2,1,0:T(8,128)(2,1)S(1)}, bf16[3,256,512]{2,1,0:T(8,128)(2,1)S(1)}, u32[]{:S(2)}, u32[]{:S(2)}) %collective-permute-start.28) | collective-permute-done | bytes 786464 | tf_op jit(solution)/shard_map/ppermute | solution.py:14
  106.4 2.3 %collective-permute-done.29.refs_4_ = bf16[3,256,512]{2,1,0:T(8,128)(2,1)S(1)} collective-permute-done((bf16[3,256,512]{2,1,0:T(8,128)(2,1)S(1)}, bf16[3,256,512]{2,1,0:T(8,128)(2,1)S(1)}, u32[]{:S(2)}, u32[]{:S(2)}) %collective-permute-start.29) | collective-permute-done | bytes 786464 | tf_op jit(solution)/shard_map/ppermute | solution.py:14
  108.7 2.2 %shard_map.149 = (bf16[1024,512]{1,0:T(8,128)(2,1)}, f32[3,256,512]{2,1,0:T(8,128)}) custom-call(s32[4]{0:T(128)S(1)} %copy-done.7, bf16[3,256,512]{2,1,0:T(8,128)(2,1)S(1)} %get-tuple-element.67.refs_1_, bf16[3,256,512]{2,1,0:T(8,128)(2,1)S(1)} %collective-permute-done.24.refs_2_, bf16[3,256,512]{2,1,0:T(8,128)(2,1)S(1)} %collective-permute-done.28.refs_3_, ...), custom_call_target="tpu_custom_call" | custom-call | flops 8 | bytes 8 | tf_op jit(solution)/shard_map/pallas_call | solution.py:115
  (27 shorter events, 0.1 us)
Async XLA Ops:
  0.6 3.8 %copy-start = (bf16[256,512]{1,0:T(8,128)(2,1)S(1)}, bf16[256,512]{1,0:T(8,128)(2,1)}, u32[]{:S(2)}) copy-start(bf16[256,512]{1,0:T(8,128)(2,1)} %refs_1_.1) | copy-start | bytes 786436
  0.6 6.8 %copy-start.6 = (s32[8,4]{0,1:T(4,128)S(1)}, s32[8,4]{0,1:T(4,128)}, u32[]{:S(2)}) copy-start(s32[8,4]{0,1:T(4,128)} %param.14) | copy-start | bytes 388
  0.7 11.0 %copy-start.5 = (bf16[1024,512]{1,0:T(8,128)(2,1)S(1)}, bf16[1024,512]{1,0:T(8,128)(2,1)}, u32[]{:S(2)}) copy-start(bf16[1024,512]{1,0:T(8,128)(2,1)} %refs_0_.4) | copy-start | bytes 3145732
  3.9 4.2 %collective-permute-start = (bf16[256,2048]{1,0:T(8,128)(2,1)S(1)}, bf16[256,2048]{1,0:T(8,128)(2,1)S(1)}, u32[]{:S(2)}, u32[]{:S(2)}) collective-permute-start(bf16[256,2048]{1,0:T(8,128)(2,1)S(1)} %get-tuple-element.44), channel_id=1, source_target_pairs={{0,1},{1,0},{2,3},{3,2},{4,5},{5,4},{6,7},{7,6},{8,9},{9,8},{10,11... | collective-permute-start | bytes 3145736 | tf_op jit(solution)/shard_map/ppermute | solution.py:14
  4.5 2.7 %collective-permute-start.1 = (bf16[256,512]{1,0:T(8,128)(2,1)S(1)}, bf16[256,512]{1,0:T(8,128)(2,1)S(1)}, u32[]{:S(2)}, u32[]{:S(2)}) collective-permute-start(bf16[256,512]{1,0:T(8,128)(2,1)S(1)} %copy-done), channel_id=1, source_target_pairs={{0,1},{1,0},{2,3},{3,2},{4,5},{5,4},{6,7},{7,6},{8,9},{9,8},{10,11... | collective-permute-start | bytes 786440 | tf_op jit(solution)/shard_map/ppermute | solution.py:14
  7.1 8.1 %collective-permute-start.11 = (bf16[256,2048]{1,0:T(8,128)(2,1)S(1)}, bf16[256,2048]{1,0:T(8,128)(2,1)S(1)}, u32[]{:S(2)}, u32[]{:S(2)}) collective-permute-start(bf16[256,2048]{1,0:T(8,128)(2,1)S(1)} %get-tuple-element.51), channel_id=1, source_target_pairs={{0,1},{1,0},{2,3},{3,2},{4,5},{5,4},{6,7},{7,6},{8,9},{9,8},{10,11... | collective-permute-start | bytes 3145736 | tf_op jit(solution)/shard_map/ppermute | solution.py:14
  8.9 22.6 %collective-permute-start.13 = (bf16[2,2,128,512]{3,2,1,0:T(8,128)(2,1)S(1)}, bf16[2,2,128,512]{3,2,1,0:T(8,128)(2,1)S(1)}, u32[]{:S(2)}, u32[]{:S(2)}) collective-permute-start(bf16[2,2,128,512]{3,2,1,0:T(8,128)(2,1)S(1)} %get-tuple-element.48), channel_id=1, source_target_pairs={{0,2},{2,0},{1,3},{3,1},{4,6},{6,4},{5,7},{7,5},{8,10},{10,8},{9,1... | collective-permute-start | bytes 1572872 | tf_op jit(solution)/shard_map/ppermute | solution.py:14
  11.6 10.2 %collective-permute-start.2 = (bf16[256,512]{1,0:T(8,128)(2,1)S(1)}, bf16[256,512]{1,0:T(8,128)(2,1)S(1)}, u32[]{:S(2)}, u32[]{:S(2)}) collective-permute-start(bf16[256,512]{1,0:T(8,128)(2,1)S(1)} %shard_map.138.refs_0_), channel_id=1, source_target_pairs={{0,8},{8,16},{16,24},{24,0},{1,9},{9,17},{17,25},{25,1},{2,10},{10... | collective-permute-start | bytes 786440 | tf_op jit(solution)/shard_map/ppermute | solution.py:14
  13.3 18.2 %collective-permute-start.6 = (bf16[256,512]{1,0:T(8,128)(2,1)S(1)}, bf16[256,512]{1,0:T(8,128)(2,1)S(1)}, u32[]{:S(2)}, u32[]{:S(2)}) collective-permute-start(bf16[256,512]{1,0:T(8,128)(2,1)S(1)} %shard_map.138.refs_0_), channel_id=1, source_target_pairs={{0,6},{2,4},{4,2},{6,0},{1,7},{3,5},{5,3},{7,1},{8,14},{10,12},{12... | collective-permute-start | bytes 786440 | tf_op jit(solution)/shard_map/ppermute | solution.py:399
  14.8 19.5 %collective-permute-start.14 = (bf16[2,2,128,512]{3,2,1,0:T(8,128)(2,1)S(1)}, bf16[2,2,128,512]{3,2,1,0:T(8,128)(2,1)S(1)}, u32[]{:S(2)}, u32[]{:S(2)}) collective-permute-start(bf16[2,2,128,512]{3,2,1,0:T(8,128)(2,1)S(1)} %get-tuple-element.53), channel_id=1, source_target_pairs={{0,4},{4,0},{1,5},{5,1},{2,6},{6,2},{3,7},{7,3},{8,12},{12,8},{9,1... | collective-permute-start | bytes 1572872 | tf_op jit(solution)/shard_map/ppermute | solution.py:14
  16.0 26.0 %collective-permute-start.12 = (bf16[2,2,128,512]{3,2,1,0:T(8,128)(2,1)S(1)}, bf16[2,2,128,512]{3,2,1,0:T(8,128)(2,1)S(1)}, u32[]{:S(2)}, u32[]{:S(2)}) collective-permute-start(bf16[2,2,128,512]{3,2,1,0:T(8,128)(2,1)S(1)} %get-tuple-element.52), channel_id=1, source_target_pairs={{0,2},{2,0},{1,3},{3,1},{4,6},{6,4},{5,7},{7,5},{8,10},{10,8},{9,1... | collective-permute-start | bytes 1572872 | tf_op jit(solution)/shard_map/ppermute | solution.py:14
  21.8 12.5 %collective-permute-start.3 = (bf16[256,512]{1,0:T(8,128)(2,1)S(1)}, bf16[256,512]{1,0:T(8,128)(2,1)S(1)}, u32[]{:S(2)}, u32[]{:S(2)}) collective-permute-start(bf16[256,512]{1,0:T(8,128)(2,1)S(1)} %collective-permute-done.2.refs_1_), channel_id=1, source_target_pairs={{0,8},{8,16},{16,24},{24,0},{1,9},{9,17},{17,25},{25,1},{2,10},{10... | collective-permute-start | bytes 786440 | tf_op jit(solution)/shard_map/ppermute | solution.py:14
  31.5 14.9 %collective-permute-start.15 = (bf16[2,2,128,512]{3,2,1,0:T(8,128)(2,1)S(1)}, bf16[2,2,128,512]{3,2,1,0:T(8,128)(2,1)S(1)}, u32[]{:S(2)}, u32[]{:S(2)}) collective-permute-start(bf16[2,2,128,512]{3,2,1,0:T(8,128)(2,1)S(1)} %get-tuple-element.58), channel_id=1, source_target_pairs={{0,4},{4,0},{1,5},{5,1},{2,6},{6,2},{3,7},{7,3},{8,12},{12,8},{9,1... | collective-permute-start | bytes 1572872 | tf_op jit(solution)/shard_map/ppermute | solution.py:14
  31.5 9.3 %collective-permute-start.7 = (bf16[256,512]{1,0:T(8,128)(2,1)S(1)}, bf16[256,512]{1,0:T(8,128)(2,1)S(1)}, u32[]{:S(2)}, u32[]{:S(2)}) collective-permute-start(bf16[256,512]{1,0:T(8,128)(2,1)S(1)} %collective-permute-done.6.refs_0_), channel_id=1, source_target_pairs={{0,8},{8,16},{16,24},{24,0},{1,9},{9,17},{17,25},{25,1},{2,10},{10... | collective-permute-start | bytes 786440 | tf_op jit(solution)/shard_map/ppermute | solution.py:14
  34.8 17.1 %collective-permute-start.18 = (bf16[2,128,512]{2,1,0:T(8,128)(2,1)S(1)}, bf16[2,128,512]{2,1,0:T(8,128)(2,1)S(1)}, u32[]{:S(2)}, u32[]{:S(2)}) collective-permute-start(bf16[2,128,512]{2,1,0:T(8,128)(2,1)S(1)} %get-tuple-element.55), channel_id=1, source_target_pairs={{0,4},{4,0},{1,5},{5,1},{2,6},{6,2},{3,7},{7,3},{8,12},{12,8},{9,1... | collective-permute-start | bytes 786440 | tf_op jit(solution)/shard_map/ppermute | solution.py:14
  40.8 12.7 %collective-permute-start.8 = (bf16[256,512]{1,0:T(8,128)(2,1)S(1)}, bf16[256,512]{1,0:T(8,128)(2,1)S(1)}, u32[]{:S(2)}, u32[]{:S(2)}) collective-permute-start(bf16[256,512]{1,0:T(8,128)(2,1)S(1)} %collective-permute-done.7.refs_1_), channel_id=1, source_target_pairs={{0,8},{8,16},{16,24},{24,0},{1,9},{9,17},{17,25},{25,1},{2,10},{10... | collective-permute-start | bytes 786440 | tf_op jit(solution)/shard_map/ppermute | solution.py:14
  40.8 14.2 %collective-permute-start.4 = (bf16[256,512]{1,0:T(8,128)(2,1)S(1)}, bf16[256,512]{1,0:T(8,128)(2,1)S(1)}, u32[]{:S(2)}, u32[]{:S(2)}) collective-permute-start(bf16[256,512]{1,0:T(8,128)(2,1)S(1)} %collective-permute-done.3.refs_2_), channel_id=1, source_target_pairs={{0,8},{8,16},{16,24},{24,0},{1,9},{9,17},{17,25},{25,1},{2,10},{10... | collective-permute-start | bytes 786440 | tf_op jit(solution)/shard_map/ppermute | solution.py:14
  42.1 13.0 %collective-permute-start.19 = (bf16[2,128,512]{2,1,0:T(8,128)(2,1)S(1)}, bf16[2,128,512]{2,1,0:T(8,128)(2,1)S(1)}, u32[]{:S(2)}, u32[]{:S(2)}) collective-permute-start(bf16[2,128,512]{2,1,0:T(8,128)(2,1)S(1)} %get-tuple-element.56), channel_id=1, source_target_pairs={{0,2},{2,0},{1,3},{3,1},{4,6},{6,4},{5,7},{7,5},{8,10},{10,8},{9,1... | collective-permute-start | bytes 786440 | tf_op jit(solution)/shard_map/ppermute | solution.py:14
  46.8 12.6 %collective-permute-start.16 = (bf16[2,128,512]{2,1,0:T(8,128)(2,1)S(1)}, bf16[2,128,512]{2,1,0:T(8,128)(2,1)S(1)}, u32[]{:S(2)}, u32[]{:S(2)}) collective-permute-start(bf16[2,128,512]{2,1,0:T(8,128)(2,1)S(1)} %get-tuple-element.59), channel_id=1, source_target_pairs={{0,4},{4,0},{1,5},{5,1},{2,6},{6,2},{3,7},{7,3},{8,12},{12,8},{9,1... | collective-permute-start | bytes 786440 | tf_op jit(solution)/shard_map/ppermute | solution.py:14
  52.0 7.5 %collective-permute-start.17 = (bf16[2,128,512]{2,1,0:T(8,128)(2,1)S(1)}, bf16[2,128,512]{2,1,0:T(8,128)(2,1)S(1)}, u32[]{:S(2)}, u32[]{:S(2)}) collective-permute-start(bf16[2,128,512]{2,1,0:T(8,128)(2,1)S(1)} %get-tuple-element.60), channel_id=1, source_target_pairs={{0,2},{2,0},{1,3},{3,1},{4,6},{6,4},{5,7},{7,5},{8,10},{10,8},{9,1... | collective-permute-start | bytes 786440 | tf_op jit(solution)/shard_map/ppermute | solution.py:14
  53.4 11.0 %collective-permute-start.9 = (bf16[256,512]{1,0:T(8,128)(2,1)S(1)}, bf16[256,512]{1,0:T(8,128)(2,1)S(1)}, u32[]{:S(2)}, u32[]{:S(2)}) collective-permute-start(bf16[256,512]{1,0:T(8,128)(2,1)S(1)} %collective-permute-done.8.refs_2_), channel_id=1, source_target_pairs={{0,8},{8,16},{16,24},{24,0},{1,9},{9,17},{17,25},{25,1},{2,10},{10... | collective-permute-start | bytes 786440 | tf_op jit(solution)/shard_map/ppermute | solution.py:14
  55.6 14.6 %collective-permute-start.21 = (bf16[256,512]{1,0:T(8,128)(2,1)S(1)}, bf16[256,512]{1,0:T(8,128)(2,1)S(1)}, u32[]{:S(2)}, u32[]{:S(2)}) collective-permute-start(bf16[256,512]{1,0:T(8,128)(2,1)S(1)} %get-tuple-element.62), channel_id=1, source_target_pairs={{0,8},{8,16},{16,24},{24,0},{1,9},{9,17},{17,25},{25,1},{2,10},{10... | collective-permute-start | bytes 786440 | tf_op jit(solution)/shard_map/ppermute | solution.py:14
  57.2 25.8 %copy-start.2 = (f32[256,512]{1,0:T(8,128)S(1)}, f32[256,512]{1,0:T(8,128)}, u32[]{:S(2)}) copy-start(f32[256,512]{1,0:T(8,128)} %master.1) | copy-start | bytes 1572868
  57.2 25.8 %copy-start.3 = (f32[256,512]{1,0:T(8,128)S(1)}, f32[256,512]{1,0:T(8,128)}, u32[]{:S(2)}) copy-start(f32[256,512]{1,0:T(8,128)} %moment_one.1) | copy-start | bytes 1572868
  57.2 25.8 %copy-start.4 = (f32[256,512]{1,0:T(8,128)S(1)}, f32[256,512]{1,0:T(8,128)}, u32[]{:S(2)}) copy-start(f32[256,512]{1,0:T(8,128)} %moment_two.1) | copy-start | bytes 1572868
  57.2 14.7 %collective-permute-start.22 = (bf16[256,512]{1,0:T(8,128)(2,1)S(1)}, bf16[256,512]{1,0:T(8,128)(2,1)S(1)}, u32[]{:S(2)}, u32[]{:S(2)}) collective-permute-start(bf16[256,512]{1,0:T(8,128)(2,1)S(1)} %get-tuple-element.63), channel_id=1, source_target_pairs={{0,24},{8,0},{16,8},{24,16},{1,25},{9,1},{17,9},{25,17},{2,26},{10... | collective-permute-start | bytes 786440 | tf_op jit(solution)/shard_map/ppermute | solution.py:14
  59.9 23.1 %collective-permute-start.23 = (bf16[256,512]{1,0:T(8,128)(2,1)S(1)}, bf16[256,512]{1,0:T(8,128)(2,1)S(1)}, u32[]{:S(2)}, u32[]{:S(2)}) collective-permute-start(bf16[256,512]{1,0:T(8,128)(2,1)S(1)} %shard_map.145), channel_id=1, source_target_pairs={{0,16},{8,24},{16,0},{24,8},{1,17},{9,25},{17,1},{25,9},{2,18},{10... | collective-permute-start | bytes 786440 | tf_op jit(solution)/shard_map/ppermute | solution.py:14
  61.4 24.8 %collective-permute-start.26 = (bf16[4,256,512]{2,1,0:T(8,128)(2,1)S(1)}, bf16[4,256,512]{2,1,0:T(8,128)(2,1)S(1)}, u32[]{:S(2)}, u32[]{:S(2)}) collective-permute-start(bf16[4,256,512]{2,1,0:T(8,128)(2,1)S(1)} %shard_map.139.refs_3_), channel_id=1, source_target_pairs={{0,4},{4,0},{1,5},{5,1},{2,6},{6,2},{3,7},{7,3},{8,12},{12,8},{9,1... | collective-permute-start | bytes 3145736 | tf_op jit(solution)/shard_map/ppermute | solution.py:14
  64.5 21.9 %collective-permute-start.20 = (bf16[4,256,512]{2,1,0:T(8,128)(2,1)S(1)}, bf16[4,256,512]{2,1,0:T(8,128)(2,1)S(1)}, u32[]{:S(2)}, u32[]{:S(2)}) collective-permute-start(bf16[4,256,512]{2,1,0:T(8,128)(2,1)S(1)} %shard_map.139.refs_3_), channel_id=1, source_target_pairs={{0,2},{2,0},{1,3},{3,1},{4,6},{6,4},{5,7},{7,5},{8,10},{10,8},{9,1... | collective-permute-start | bytes 3145736 | tf_op jit(solution)/shard_map/ppermute | solution.py:14
  65.1 27.2 %copy-start.1 = (bf16[256,8192]{1,0:T(8,128)(2,1)S(1)}, bf16[256,8192]{1,0:T(8,128)(2,1)}, u32[]{:S(2)}) copy-start(bf16[256,8192]{1,0:T(8,128)(2,1)} %refs_0_.5) | copy-start | bytes 12582916
  83.9 2.4 %collective-permute-start.24 = (bf16[3,256,512]{2,1,0:T(8,128)(2,1)S(1)}, bf16[3,256,512]{2,1,0:T(8,128)(2,1)S(1)}, u32[]{:S(2)}, u32[]{:S(2)}) collective-permute-start(bf16[3,256,512]{2,1,0:T(8,128)(2,1)S(1)} %get-tuple-element.67.refs_1_), channel_id=1, source_target_pairs={{0,1},{1,0},{2,3},{3,2},{4,5},{5,4},{6,7},{7,6},{8,9},{9,8},{10,11... | collective-permute-start | bytes 2359304 | tf_op jit(solution)/shard_map/ppermute | solution.py:14
  84.0 5.0 %collective-permute-start.5 = (bf16[4,256,512]{2,1,0:T(8,128)(2,1)S(1)}, bf16[4,256,512]{2,1,0:T(8,128)(2,1)S(1)}, u32[]{:S(2)}, u32[]{:S(2)}) collective-permute-start(bf16[4,256,512]{2,1,0:T(8,128)(2,1)S(1)} %shard_map.139.refs_3_), channel_id=1, source_target_pairs={{0,1},{1,0},{2,3},{3,2},{4,5},{5,4},{6,7},{7,6},{8,9},{9,8},{10,11... | collective-permute-start | bytes 3145736 | tf_op jit(solution)/shard_map/ppermute | solution.py:14
  84.5 4.8 %collective-permute-start.10 = (bf16[4,256,512]{2,1,0:T(8,128)(2,1)S(1)}, bf16[4,256,512]{2,1,0:T(8,128)(2,1)S(1)}, u32[]{:S(2)}, u32[]{:S(2)}) collective-permute-start(bf16[4,256,512]{2,1,0:T(8,128)(2,1)S(1)} %shard_map.140.refs_5_), channel_id=1, source_target_pairs={{0,1},{1,0},{2,3},{3,2},{4,5},{5,4},{6,7},{7,6},{8,9},{9,8},{10,11... | collective-permute-start | bytes 3145736 | tf_op jit(solution)/shard_map/ppermute | solution.py:14
  86.3 4.5 %collective-permute-start.27 = (bf16[4,256,512]{2,1,0:T(8,128)(2,1)S(1)}, bf16[4,256,512]{2,1,0:T(8,128)(2,1)S(1)}, u32[]{:S(2)}, u32[]{:S(2)}) collective-permute-start(bf16[4,256,512]{2,1,0:T(8,128)(2,1)S(1)} %collective-permute-done.26.refs_9_), channel_id=1, source_target_pairs={{0,1},{1,0},{2,3},{3,2},{4,5},{5,4},{6,7},{7,6},{8,9},{9,8},{10,11... | collective-permute-start | bytes 3145736 | tf_op jit(solution)/shard_map/ppermute | solution.py:14
  86.4 5.9 %collective-permute-start.25 = (bf16[4,256,512]{2,1,0:T(8,128)(2,1)S(1)}, bf16[4,256,512]{2,1,0:T(8,128)(2,1)S(1)}, u32[]{:S(2)}, u32[]{:S(2)}) collective-permute-start(bf16[4,256,512]{2,1,0:T(8,128)(2,1)S(1)} %collective-permute-done.20.refs_7_), channel_id=1, source_target_pairs={{0,1},{1,0},{2,3},{3,2},{4,5},{5,4},{6,7},{7,6},{8,9},{9,8},{10,11... | collective-permute-start | bytes 3145736 | tf_op jit(solution)/shard_map/ppermute | solution.py:14
  86.8 19.6 %collective-permute-start.28 = (bf16[3,256,512]{2,1,0:T(8,128)(2,1)S(1)}, bf16[3,256,512]{2,1,0:T(8,128)(2,1)S(1)}, u32[]{:S(2)}, u32[]{:S(2)}) collective-permute-start(bf16[3,256,512]{2,1,0:T(8,128)(2,1)S(1)} %get-tuple-element.67.refs_1_), channel_id=1, source_target_pairs={{0,2},{2,0},{1,3},{3,1},{4,6},{6,4},{5,7},{7,5},{8,10},{10,8},{9,1... | collective-permute-start | bytes 2359304 | tf_op jit(solution)/shard_map/ppermute | solution.py:14
  92.3 16.4 %copy-start.7 = (s32[4]{0:T(128)S(1)}, s32[4]{0:T(128)}, u32[]{:S(2)}) copy-start(s32[4]{0:T(128)} %refs_0_.6) | copy-start | bytes 52
  106.4 2.3 %collective-permute-start.29 = (bf16[3,256,512]{2,1,0:T(8,128)(2,1)S(1)}, bf16[3,256,512]{2,1,0:T(8,128)(2,1)S(1)}, u32[]{:S(2)}, u32[]{:S(2)}) collective-permute-start(bf16[3,256,512]{2,1,0:T(8,128)(2,1)S(1)} %collective-permute-done.28.refs_3_), channel_id=1, source_target_pairs={{0,1},{1,0},{2,3},{3,2},{4,5},{5,4},{6,7},{7,6},{8,9},{9,8},{10,11... | collective-permute-start | bytes 2359304 | tf_op jit(solution)/shard_map/ppermute | solution.py:14
